TPU v7x, 512 devices: a whole 4x8x8 slice. The times are simulated.
512 devices in a mesh: chan: 128 (over z, y, core), cuts: 4 (over x).
Axes of the slice: x: 4, y: 8, z: 8, core: 2. Of those that a mesh axis runs over, the one named last changes fastest.
Arguments:
- strain: bfloat16 [4, 4096, 8192], P('cuts', 'chan'), may hold values from -6 to 6
- band_taper: float32 [960], replicated, may hold values from 0.5 to 2
- pair_list: int32 [128, 6, 2], P('chan'), may hold values from 0 to 127, as said below
- pair_counts: int32 [128], P('chan'), may hold values from 1 to 6, as said below
Outputs:
- lag_stacks: bfloat16 [2048, 768, 32], P('cuts', 'chan')
Inputs may be any that keep to these rules, and one draw needn't show every extreme that they name: `pair_list`: both blocks of every slot of owner b, padded ones too, lie within 8 blocks of b; some owner has a source block exactly 8 above it and some owner a target block exactly 8 below it. `pair_counts`: some owner has 6 live slots and some owner one.
All inputs are finite; a program needn't handle non-finite values.
Results may differ from a plain program's by a relative error of at most 0.0065.
Values may be sent and summed in bfloat16 or wider, within the bound.
A program may use at most 64 MiB of HBM per device.

v0:
```python
import math

import jax
import jax.numpy as jnp
from jax import lax
from jax.sharding import PartitionSpec as P

SAMP = 8192
STRIDE = 4
F0 = 32
NF = 960
SMOOTH = 32
LAG = 1024


def shifted(value, axis, steps):
    count = lax.axis_size(axis)
    leading, last = (max(0, -steps), min(count, count - steps))
    return lax.ppermute(value, axis, [(source, source + steps) for source in range(leading, last)])


def band_table(offset, length):
    sample_ids = offset + jnp.arange(length, dtype=jnp.int32)
    bin_ids = F0 + jnp.arange(NF, dtype=jnp.int32)
    phases = sample_ids[:, None] * bin_ids[None, :] % SAMP
    angles = phases.astype(jnp.float32) * (2.0 * math.pi / SAMP)
    return jnp.concatenate([jnp.cos(angles), -jnp.sin(angles)], axis=1).astype(jnp.bfloat16)


def spectrum(signal):
    block_len = min(512, SAMP)

    def advance(turn, summed):
        piece = lax.dynamic_slice_in_dim(signal, turn * block_len, block_len, 1)
        return summed + jnp.dot(
            piece, band_table(turn * block_len, block_len), preferred_element_type=jnp.float32
        )

    initial = jnp.zeros((signal.shape[0], 2 * NF), jnp.float32)
    return lax.fori_loop(0, SAMP // block_len, advance, initial)


def whiten(spectra, band_taper):
    real_part = spectra[:, :NF]
    imag_part = spectra[:, NF:]
    magnitude = jnp.sqrt(real_part * real_part + imag_part * imag_part)
    bin_ids = jnp.arange(NF, dtype=jnp.int32)
    window = (jnp.abs(bin_ids[:, None] - bin_ids[None, :]) <= SMOOTH).astype(jnp.float32)
    level = jnp.dot(magnitude, window, precision=lax.Precision.HIGHEST) / jnp.sum(window, axis=0)
    factor = band_taper / (level + 1e-06)
    return jnp.concatenate([real_part * factor, imag_part * factor], axis=1).astype(jnp.bfloat16)


def cross_spectrum(source, target):
    src_real = source[..., :NF]
    src_imag = source[..., NF:]
    tgt_real = target[..., :NF]
    tgt_imag = target[..., NF:]
    return jnp.concatenate(
        [src_real * tgt_real + src_imag * tgt_imag, src_imag * tgt_real - src_real * tgt_imag],
        axis=-1,
    )


def lag_table(lag_begin, lag_count):
    lag_ids = lag_begin + jnp.arange(lag_count, dtype=jnp.int32) - LAG + SAMP
    bin_ids = F0 + jnp.arange(NF, dtype=jnp.int32)
    phases = bin_ids[:, None] * (lag_ids[None, :] * STRIDE) % SAMP
    angles = phases.astype(jnp.float32) * (2.0 * math.pi / SAMP)
    scale = 1.0 / math.sqrt(NF)
    return jnp.concatenate([jnp.cos(angles) * scale, -jnp.sin(angles) * scale], axis=0)


def lag_rows(spectra, lag_begin, lag_count):
    return jnp.einsum(
        "pcf,ft->tpc", spectra, lag_table(lag_begin, lag_count), precision=lax.Precision.HIGHEST
    )


def shards(strain, band_taper, pair_list, pair_counts):
    whitened = whiten(spectrum(strain[0]), band_taper)
    reach = min(8, lax.axis_size("chan") // 4)
    owner = lax.axis_index("chan")
    nearby = []
    for distance in range(-reach, reach + 1):
        if distance == 0:
            nearby.append(whitened)
        else:
            nearby.append(shifted(whitened, "chan", -distance))
    window_blocks = jnp.stack(nearby)
    slots = pair_list[0]
    block_ids = jnp.arange(2 * reach + 1, dtype=jnp.int32) - reach + owner
    source_pick = (slots[:, 0:1] == block_ids[None, :]).astype(jnp.bfloat16)
    target_pick = (slots[:, 1:2] == block_ids[None, :]).astype(jnp.bfloat16)
    sources = jnp.einsum(
        "pw,wcf->pcf", source_pick, window_blocks, preferred_element_type=jnp.float32
    )
    targets = jnp.einsum(
        "pw,wcf->pcf", target_pick, window_blocks, preferred_element_type=jnp.float32
    )
    slot_count = slots.shape[0]
    live = (jnp.arange(slot_count, dtype=jnp.int32) < pair_counts[0]).astype(jnp.float32)
    cross = cross_spectrum(sources, targets) * live[:, None, None]
    quarter = 2 * LAG // lax.axis_size("cuts")

    def one_block(turn):
        return lag_rows(cross, turn * quarter, quarter)

    pieces = lax.map(
        one_block, jnp.arange(lax.axis_size("cuts") * quarter // quarter, dtype=jnp.int32)
    )
    stacks = lax.psum_scatter(
        pieces.reshape(lax.axis_size("cuts") * quarter, cross.shape[0], cross.shape[1]),
        "cuts",
        scatter_dimension=0,
        tiled=True,
    )
    return stacks.astype(jnp.bfloat16)


def solution(mesh):
    in_specs = (P("cuts", "chan", None), P(), P("chan", None, None), P("chan"))
    out_specs = P("cuts", "chan", None)
    return jax.shard_map(shards, mesh=mesh, in_specs=in_specs, out_specs=out_specs, check_vma=False)
```

profile of v0, /device:TPU:1, one launch (start us, length us, event | category | flops | bytes accessed | tf_op | source)
XLA Modules:
  0.0 378.1 jit_solution(70880169758779087)
XLA Ops:
  6.7 167.4 %while.31 = (s32[]{:T(128)}, f32[32,1920]{1,0:T(8,128)S(1)}, bf16[32,8192]{1,0:T(8,128)(2,1)}, s32[]{:T(128)}, s32[]{:T(128)}, /*index=5*/s32[]{:T(128)}, s32[]{:T(128)}) while((s32[]{:T(128)}, f32[32,1920]{1,0:T(8,128)S(1)}, bf16[32,8192]{1,0:T(8,128)(2,1)}, s32[]{:T(128)}, s32[]{:T(128)}, /*index=5*/s32[]{:T(128)}, ...), condition=%wide.region_1.2_spmd.clone, body=%wide.region_0.1_spmd.clone.sunk | while | flops 75326920 | bytes 4468365 | solution.py:40
  6.8 9.0 %cosine_convert_fusion.2 = (bf16[512,960]{1,0:T(8,128)(2,1)S(1)}, bf16[512,960]{1,0:T(8,128)(2,1)S(1)}) fusion(s32[960]{0:T(1024)S(1)} %iota_add_fusion.7, s32[512]{0:T(512)S(1)} %iota_add_fusion.8), kind=kLoop, calls=%fused_computation.28.clone.1 | loop fusion | flops 8355840 | bytes 1971968 | tf_op jit(solution)/shard_map/convert
  17.2 9.0 %cosine_convert_fusion.2 = (bf16[512,960]{1,0:T(8,128)(2,1)S(1)}, bf16[512,960]{1,0:T(8,128)(2,1)S(1)}) fusion(s32[960]{0:T(1024)S(1)} %iota_add_fusion.7, s32[512]{0:T(512)S(1)} %iota_add_fusion.8), kind=kLoop, calls=%fused_computation.28.clone.1 | loop fusion | flops 8355840 | bytes 1971968 | tf_op jit(solution)/shard_map/convert
  27.7 9.0 %cosine_convert_fusion.2 = (bf16[512,960]{1,0:T(8,128)(2,1)S(1)}, bf16[512,960]{1,0:T(8,128)(2,1)S(1)}) fusion(s32[960]{0:T(1024)S(1)} %iota_add_fusion.7, s32[512]{0:T(512)S(1)} %iota_add_fusion.8), kind=kLoop, calls=%fused_computation.28.clone.1 | loop fusion | flops 8355840 | bytes 1971968 | tf_op jit(solution)/shard_map/convert
  38.2 9.0 %cosine_convert_fusion.2 = (bf16[512,960]{1,0:T(8,128)(2,1)S(1)}, bf16[512,960]{1,0:T(8,128)(2,1)S(1)}) fusion(s32[960]{0:T(1024)S(1)} %iota_add_fusion.7, s32[512]{0:T(512)S(1)} %iota_add_fusion.8), kind=kLoop, calls=%fused_computation.28.clone.1 | loop fusion | flops 8355840 | bytes 1971968 | tf_op jit(solution)/shard_map/convert
  48.6 9.0 %cosine_convert_fusion.2 = (bf16[512,960]{1,0:T(8,128)(2,1)S(1)}, bf16[512,960]{1,0:T(8,128)(2,1)S(1)}) fusion(s32[960]{0:T(1024)S(1)} %iota_add_fusion.7, s32[512]{0:T(512)S(1)} %iota_add_fusion.8), kind=kLoop, calls=%fused_computation.28.clone.1 | loop fusion | flops 8355840 | bytes 1971968 | tf_op jit(solution)/shard_map/convert
  59.1 9.0 %cosine_convert_fusion.2 = (bf16[512,960]{1,0:T(8,128)(2,1)S(1)}, bf16[512,960]{1,0:T(8,128)(2,1)S(1)}) fusion(s32[960]{0:T(1024)S(1)} %iota_add_fusion.7, s32[512]{0:T(512)S(1)} %iota_add_fusion.8), kind=kLoop, calls=%fused_computation.28.clone.1 | loop fusion | flops 8355840 | bytes 1971968 | tf_op jit(solution)/shard_map/convert
  69.5 9.0 %cosine_convert_fusion.2 = (bf16[512,960]{1,0:T(8,128)(2,1)S(1)}, bf16[512,960]{1,0:T(8,128)(2,1)S(1)}) fusion(s32[960]{0:T(1024)S(1)} %iota_add_fusion.7, s32[512]{0:T(512)S(1)} %iota_add_fusion.8), kind=kLoop, calls=%fused_computation.28.clone.1 | loop fusion | flops 8355840 | bytes 1971968 | tf_op jit(solution)/shard_map/convert
  80.0 9.0 %cosine_convert_fusion.2 = (bf16[512,960]{1,0:T(8,128)(2,1)S(1)}, bf16[512,960]{1,0:T(8,128)(2,1)S(1)}) fusion(s32[960]{0:T(1024)S(1)} %iota_add_fusion.7, s32[512]{0:T(512)S(1)} %iota_add_fusion.8), kind=kLoop, calls=%fused_computation.28.clone.1 | loop fusion | flops 8355840 | bytes 1971968 | tf_op jit(solution)/shard_map/convert
  90.5 9.0 %cosine_convert_fusion.2 = (bf16[512,960]{1,0:T(8,128)(2,1)S(1)}, bf16[512,960]{1,0:T(8,128)(2,1)S(1)}) fusion(s32[960]{0:T(1024)S(1)} %iota_add_fusion.7, s32[512]{0:T(512)S(1)} %iota_add_fusion.8), kind=kLoop, calls=%fused_computation.28.clone.1 | loop fusion | flops 8355840 | bytes 1971968 | tf_op jit(solution)/shard_map/convert
  100.9 9.0 %cosine_convert_fusion.2 = (bf16[512,960]{1,0:T(8,128)(2,1)S(1)}, bf16[512,960]{1,0:T(8,128)(2,1)S(1)}) fusion(s32[960]{0:T(1024)S(1)} %iota_add_fusion.7, s32[512]{0:T(512)S(1)} %iota_add_fusion.8), kind=kLoop, calls=%fused_computation.28.clone.1 | loop fusion | flops 8355840 | bytes 1971968 | tf_op jit(solution)/shard_map/convert
  111.4 9.0 %cosine_convert_fusion.2 = (bf16[512,960]{1,0:T(8,128)(2,1)S(1)}, bf16[512,960]{1,0:T(8,128)(2,1)S(1)}) fusion(s32[960]{0:T(1024)S(1)} %iota_add_fusion.7, s32[512]{0:T(512)S(1)} %iota_add_fusion.8), kind=kLoop, calls=%fused_computation.28.clone.1 | loop fusion | flops 8355840 | bytes 1971968 | tf_op jit(solution)/shard_map/convert
  121.8 9.0 %cosine_convert_fusion.2 = (bf16[512,960]{1,0:T(8,128)(2,1)S(1)}, bf16[512,960]{1,0:T(8,128)(2,1)S(1)}) fusion(s32[960]{0:T(1024)S(1)} %iota_add_fusion.7, s32[512]{0:T(512)S(1)} %iota_add_fusion.8), kind=kLoop, calls=%fused_computation.28.clone.1 | loop fusion | flops 8355840 | bytes 1971968 | tf_op jit(solution)/shard_map/convert
  132.3 9.0 %cosine_convert_fusion.2 = (bf16[512,960]{1,0:T(8,128)(2,1)S(1)}, bf16[512,960]{1,0:T(8,128)(2,1)S(1)}) fusion(s32[960]{0:T(1024)S(1)} %iota_add_fusion.7, s32[512]{0:T(512)S(1)} %iota_add_fusion.8), kind=kLoop, calls=%fused_computation.28.clone.1 | loop fusion | flops 8355840 | bytes 1971968 | tf_op jit(solution)/shard_map/convert
  142.8 9.0 %cosine_convert_fusion.2 = (bf16[512,960]{1,0:T(8,128)(2,1)S(1)}, bf16[512,960]{1,0:T(8,128)(2,1)S(1)}) fusion(s32[960]{0:T(1024)S(1)} %iota_add_fusion.7, s32[512]{0:T(512)S(1)} %iota_add_fusion.8), kind=kLoop, calls=%fused_computation.28.clone.1 | loop fusion | flops 8355840 | bytes 1971968 | tf_op jit(solution)/shard_map/convert
  153.2 9.0 %cosine_convert_fusion.2 = (bf16[512,960]{1,0:T(8,128)(2,1)S(1)}, bf16[512,960]{1,0:T(8,128)(2,1)S(1)}) fusion(s32[960]{0:T(1024)S(1)} %iota_add_fusion.7, s32[512]{0:T(512)S(1)} %iota_add_fusion.8), kind=kLoop, calls=%fused_computation.28.clone.1 | loop fusion | flops 8355840 | bytes 1971968 | tf_op jit(solution)/shard_map/convert
  163.7 9.0 %cosine_convert_fusion.2 = (bf16[512,960]{1,0:T(8,128)(2,1)S(1)}, bf16[512,960]{1,0:T(8,128)(2,1)S(1)}) fusion(s32[960]{0:T(1024)S(1)} %iota_add_fusion.7, s32[512]{0:T(512)S(1)} %iota_add_fusion.8), kind=kLoop, calls=%fused_computation.28.clone.1 | loop fusion | flops 8355840 | bytes 1971968 | tf_op jit(solution)/shard_map/convert
  174.9 8.3 %collective-permute-start = (bf16[32,1920]{1,0:T(8,128)(2,1)S(1)}, bf16[32,1920]{1,0:T(8,128)(2,1)S(1)}, u32[]{:S(2)}, u32[]{:S(2)}) collective-permute-start(bf16[32,1920]{1,0:T(8,128)(2,1)S(1)} %pad_maximum_fusion), channel_id=1, source_target_pairs={{0,32},{4,36},{8,40},{12,44},{16,48},{20,52},{24,56},{28,60},{32,6... | collective-permute-start | bytes 368648 | tf_op jit(solution)/shard_map/ppermute | solution.py:19
  183.2 4.4 %collective-permute-start.1 = (bf16[32,1920]{1,0:T(8,128)(2,1)S(1)}, bf16[32,1920]{1,0:T(8,128)(2,1)S(1)}, u32[]{:S(2)}, u32[]{:S(2)}) collective-permute-start(bf16[32,1920]{1,0:T(8,128)(2,1)S(1)} %pad_maximum_fusion), channel_id=1, source_target_pairs={{0,28},{4,32},{8,36},{12,40},{16,44},{20,48},{24,52},{28,56},{32,6... | collective-permute-start | bytes 368648 | tf_op jit(solution)/shard_map/ppermute | solution.py:19
  187.6 5.2 %collective-permute-start.2 = (bf16[32,1920]{1,0:T(8,128)(2,1)S(1)}, bf16[32,1920]{1,0:T(8,128)(2,1)S(1)}, u32[]{:S(2)}, u32[]{:S(2)}) collective-permute-start(bf16[32,1920]{1,0:T(8,128)(2,1)S(1)} %pad_maximum_fusion), channel_id=1, source_target_pairs={{0,24},{4,28},{8,32},{12,36},{16,40},{20,44},{24,48},{28,52},{32,5... | collective-permute-start | bytes 368648 | tf_op jit(solution)/shard_map/ppermute | solution.py:19
  192.9 4.2 %collective-permute-start.3 = (bf16[32,1920]{1,0:T(8,128)(2,1)S(1)}, bf16[32,1920]{1,0:T(8,128)(2,1)S(1)}, u32[]{:S(2)}, u32[]{:S(2)}) collective-permute-start(bf16[32,1920]{1,0:T(8,128)(2,1)S(1)} %pad_maximum_fusion), channel_id=1, source_target_pairs={{0,20},{4,24},{8,28},{12,32},{16,36},{20,40},{24,44},{28,48},{32,5... | collective-permute-start | bytes 368648 | tf_op jit(solution)/shard_map/ppermute | solution.py:19
  197.1 2.4 collective-permute-start.4
  200.3 5.1 %collective-permute-start.5 = (bf16[32,1920]{1,0:T(8,128)(2,1)S(1)}, bf16[32,1920]{1,0:T(8,128)(2,1)S(1)}, u32[]{:S(2)}, u32[]{:S(2)}) collective-permute-start(bf16[32,1920]{1,0:T(8,128)(2,1)S(1)} %pad_maximum_fusion), channel_id=1, source_target_pairs={{0,12},{4,16},{8,20},{12,24},{16,28},{20,32},{24,36},{28,40},{32,4... | collective-permute-start | bytes 368648 | tf_op jit(solution)/shard_map/ppermute | solution.py:19
  205.4 3.2 collective-permute-start.6
  208.6 1.9 collective-permute-start.7
  210.6 2.4 collective-permute-start.8
  215.0 4.5 %collective-permute-done.5 = bf16[32,1920]{1,0:T(8,128)(2,1)S(1)} collective-permute-done((bf16[32,1920]{1,0:T(8,128)(2,1)S(1)}, bf16[32,1920]{1,0:T(8,128)(2,1)S(1)}, u32[]{:S(2)}, u32[]{:S(2)}) %collective-permute-start.5) | collective-permute-done | bytes 122912 | tf_op jit(solution)/shard_map/ppermute | solution.py:19
  220.8 1.6 collective-permute-done.6
  227.7 4.3 %collective-permute-done.10 = bf16[32,1920]{1,0:T(8,128)(2,1)S(1)} collective-permute-done((bf16[32,1920]{1,0:T(8,128)(2,1)S(1)}, bf16[32,1920]{1,0:T(8,128)(2,1)S(1)}, u32[]{:S(2)}, u32[]{:S(2)}) %collective-permute-start.10) | collective-permute-done | bytes 122912 | tf_op jit(solution)/shard_map/ppermute | solution.py:19
  233.3 4.2 %collective-permute-done.11 = bf16[32,1920]{1,0:T(8,128)(2,1)S(1)} collective-permute-done((bf16[32,1920]{1,0:T(8,128)(2,1)S(1)}, bf16[32,1920]{1,0:T(8,128)(2,1)S(1)}, u32[]{:S(2)}, u32[]{:S(2)}) %collective-permute-start.11) | collective-permute-done | bytes 122912 | tf_op jit(solution)/shard_map/ppermute | solution.py:19
  237.5 5.1 %collective-permute-done.12 = bf16[32,1920]{1,0:T(8,128)(2,1)S(1)} collective-permute-done((bf16[32,1920]{1,0:T(8,128)(2,1)S(1)}, bf16[32,1920]{1,0:T(8,128)(2,1)S(1)}, u32[]{:S(2)}, u32[]{:S(2)}) %collective-permute-start.12) | collective-permute-done | bytes 122912 | tf_op jit(solution)/shard_map/ppermute | solution.py:19
  242.7 2.5 collective-permute-done.13
  249.4 66.2 %while.30 = (s32[]{:T(128)}, f32[4,512,6,32]{1,0,3,2:T(4,128)S(1)}, s32[4]{0:T(128)S(1)}, f32[6,32,1920]{2,1,0:T(8,128)S(1)}, s32[]{:T(128)}, /*index=5*/s32[1]{0:T(128)}, s32[]{:T(128)}) while((s32[]{:T(128)}, f32[4,512,6,32]{1,0,3,2:T(4,128)S(1)}, s32[4]{0:T(128)S(1)}, f32[6,32,1920]{2,1,0:T(8,128)S(1)}, s32[]{:T(128)}, ...), condition=%wide.region_4.5_spmd, body=%wide.region_3.4_spmd.sunk | while | flops 2274265600 | bytes 11316845 | solution.py:109
  250.9 7.8 %cosine_multiply_fusion.2 = (f32[960,512]{1,0:T(8,128)S(1)}, f32[960,512]{1,0:T(8,128)S(1)}) fusion(s32[512]{0:T(512)S(1)} %add_multiply_fusion.2, s32[960]{0:T(1024)S(1)} %iota_add_fusion.6), kind=kLoop, calls=%fused_computation.13.clone.1 | loop fusion | flops 8355840 | bytes 3938048 | tf_op jit(solution)/shard_map/while/body/eval_jaxpr/mul | solution.py:71
  258.7 3.1 fusion.47
  262.3 3.8 %dynamic_update_slice.11 = f32[4,512,6,32]{1,0,3,2:T(4,128)S(1)} dynamic-update-slice(f32[4,512,6,32]{1,0,3,2:T(4,128)S(1)} %get-tuple-element.307, f32[1,512,6,32]{1,0,3,2:T(1,128)S(1)} %copy.21, s32[]{:T(128)} %get-tuple-element.306, s32[]{:T(128)} %constant.189.clone.1..sunk, s32[]{:T(128)} %constant.189.clone.1..sunk, s32[]{:T(128)} %constant.189.clone.1..sunk) | dynamic-update-slice | bytes 786436 | tf_op jit(solution)/shard_map/while/body/jit(dynamic_update_index_in_dim)/dynamic_update_slice | solution.py:109
  267.4 7.8 %cosine_multiply_fusion.2 = (f32[960,512]{1,0:T(8,128)S(1)}, f32[960,512]{1,0:T(8,128)S(1)}) fusion(s32[512]{0:T(512)S(1)} %add_multiply_fusion.2, s32[960]{0:T(1024)S(1)} %iota_add_fusion.6), kind=kLoop, calls=%fused_computation.13.clone.1 | loop fusion | flops 8355840 | bytes 3938048 | tf_op jit(solution)/shard_map/while/body/eval_jaxpr/mul | solution.py:71
  275.2 3.1 fusion.47
  278.8 3.8 %dynamic_update_slice.11 = f32[4,512,6,32]{1,0,3,2:T(4,128)S(1)} dynamic-update-slice(f32[4,512,6,32]{1,0,3,2:T(4,128)S(1)} %get-tuple-element.307, f32[1,512,6,32]{1,0,3,2:T(1,128)S(1)} %copy.21, s32[]{:T(128)} %get-tuple-element.306, s32[]{:T(128)} %constant.189.clone.1..sunk, s32[]{:T(128)} %constant.189.clone.1..sunk, s32[]{:T(128)} %constant.189.clone.1..sunk) | dynamic-update-slice | bytes 786436 | tf_op jit(solution)/shard_map/while/body/jit(dynamic_update_index_in_dim)/dynamic_update_slice | solution.py:109
  283.9 7.8 %cosine_multiply_fusion.2 = (f32[960,512]{1,0:T(8,128)S(1)}, f32[960,512]{1,0:T(8,128)S(1)}) fusion(s32[512]{0:T(512)S(1)} %add_multiply_fusion.2, s32[960]{0:T(1024)S(1)} %iota_add_fusion.6), kind=kLoop, calls=%fused_computation.13.clone.1 | loop fusion | flops 8355840 | bytes 3938048 | tf_op jit(solution)/shard_map/while/body/eval_jaxpr/mul | solution.py:71
  291.8 3.1 fusion.47
  295.3 3.8 %dynamic_update_slice.11 = f32[4,512,6,32]{1,0,3,2:T(4,128)S(1)} dynamic-update-slice(f32[4,512,6,32]{1,0,3,2:T(4,128)S(1)} %get-tuple-element.307, f32[1,512,6,32]{1,0,3,2:T(1,128)S(1)} %copy.21, s32[]{:T(128)} %get-tuple-element.306, s32[]{:T(128)} %constant.189.clone.1..sunk, s32[]{:T(128)} %constant.189.clone.1..sunk, s32[]{:T(128)} %constant.189.clone.1..sunk) | dynamic-update-slice | bytes 786436 | tf_op jit(solution)/shard_map/while/body/jit(dynamic_update_index_in_dim)/dynamic_update_slice | solution.py:109
  300.4 7.8 %cosine_multiply_fusion.2 = (f32[960,512]{1,0:T(8,128)S(1)}, f32[960,512]{1,0:T(8,128)S(1)}) fusion(s32[512]{0:T(512)S(1)} %add_multiply_fusion.2, s32[960]{0:T(1024)S(1)} %iota_add_fusion.6), kind=kLoop, calls=%fused_computation.13.clone.1 | loop fusion | flops 8355840 | bytes 3938048 | tf_op jit(solution)/shard_map/while/body/eval_jaxpr/mul | solution.py:71
  308.3 3.1 fusion.47
  311.8 3.8 %dynamic_update_slice.11 = f32[4,512,6,32]{1,0,3,2:T(4,128)S(1)} dynamic-update-slice(f32[4,512,6,32]{1,0,3,2:T(4,128)S(1)} %get-tuple-element.307, f32[1,512,6,32]{1,0,3,2:T(1,128)S(1)} %copy.21, s32[]{:T(128)} %get-tuple-element.306, s32[]{:T(128)} %constant.189.clone.1..sunk, s32[]{:T(128)} %constant.189.clone.1..sunk, s32[]{:T(128)} %constant.189.clone.1..sunk) | dynamic-update-slice | bytes 786436 | tf_op jit(solution)/shard_map/while/body/jit(dynamic_update_index_in_dim)/dynamic_update_slice | solution.py:109
  315.6 2.2 reshape.68
  317.9 51.6 %reduce-scatter.2.cloned.1.call-done = f32[512,6,32]{0,2,1:T(8,128)} async-done(((f32[2048,6,32]{0,2,1:T(8,128)}), f32[512,6,32]{0,2,1:T(8,128)}) %reduce-scatter.2.cloned.1.call-update) | async-done | bytes 393232 | tf_op jit(solution)/shard_map/reduce_scatter | solution.py:112
  369.5 1.7 convert_element_type.52
  (118 shorter events, 41.4 us)
Async XLA Ops:
  6.5 363.0 %reduce-scatter.2.cloned.1.call-start = ((), (), s32[]{:S(2)}) async-start(), calls=%async_computation.1 | async-start | bytes 1966080 | tf_op jit(solution)/shard_map/reduce_scatter | solution.py:112
  6.7 167.4 %copy-start.1 = (f32[960]{0:T(1024)S(1)}, f32[960]{0:T(1024)}, u32[]{:S(2)}) copy-start(f32[960]{0:T(1024)} %param.9) | copy-start | bytes 11524
  174.1 25.4 %copy-start = (s32[1,6,2]{1,2,0:T(2,128)S(1)}, s32[1,6,2]{1,2,0:T(2,128)}, u32[]{:S(2)}) copy-start(s32[1,6,2]{1,2,0:T(2,128)} %param.10) | copy-start | bytes 148
  174.9 25.3 %collective-permute-start = (bf16[32,1920]{1,0:T(8,128)(2,1)S(1)}, bf16[32,1920]{1,0:T(8,128)(2,1)S(1)}, u32[]{:S(2)}, u32[]{:S(2)}) collective-permute-start(bf16[32,1920]{1,0:T(8,128)(2,1)S(1)} %pad_maximum_fusion), channel_id=1, source_target_pairs={{0,32},{4,36},{8,40},{12,44},{16,48},{20,52},{24,56},{28,60},{32,6... | collective-permute-start | bytes 368648 | tf_op jit(solution)/shard_map/ppermute | solution.py:19
  183.2 22.1 %collective-permute-start.1 = (bf16[32,1920]{1,0:T(8,128)(2,1)S(1)}, bf16[32,1920]{1,0:T(8,128)(2,1)S(1)}, u32[]{:S(2)}, u32[]{:S(2)}) collective-permute-start(bf16[32,1920]{1,0:T(8,128)(2,1)S(1)} %pad_maximum_fusion), channel_id=1, source_target_pairs={{0,28},{4,32},{8,36},{12,40},{16,44},{20,48},{24,52},{28,56},{32,6... | collective-permute-start | bytes 368648 | tf_op jit(solution)/shard_map/ppermute | solution.py:19
  187.6 21.0 %collective-permute-start.2 = (bf16[32,1920]{1,0:T(8,128)(2,1)S(1)}, bf16[32,1920]{1,0:T(8,128)(2,1)S(1)}, u32[]{:S(2)}, u32[]{:S(2)}) collective-permute-start(bf16[32,1920]{1,0:T(8,128)(2,1)S(1)} %pad_maximum_fusion), channel_id=1, source_target_pairs={{0,24},{4,28},{8,32},{12,36},{16,40},{20,44},{24,48},{28,52},{32,5... | collective-permute-start | bytes 368648 | tf_op jit(solution)/shard_map/ppermute | solution.py:19
  192.9 17.7 %collective-permute-start.3 = (bf16[32,1920]{1,0:T(8,128)(2,1)S(1)}, bf16[32,1920]{1,0:T(8,128)(2,1)S(1)}, u32[]{:S(2)}, u32[]{:S(2)}) collective-permute-start(bf16[32,1920]{1,0:T(8,128)(2,1)S(1)} %pad_maximum_fusion), channel_id=1, source_target_pairs={{0,20},{4,24},{8,28},{12,32},{16,36},{20,40},{24,44},{28,48},{32,5... | collective-permute-start | bytes 368648 | tf_op jit(solution)/shard_map/ppermute | solution.py:19
  197.1 16.6 %collective-permute-start.4 = (bf16[32,1920]{1,0:T(8,128)(2,1)S(1)}, bf16[32,1920]{1,0:T(8,128)(2,1)S(1)}, u32[]{:S(2)}, u32[]{:S(2)}) collective-permute-start(bf16[32,1920]{1,0:T(8,128)(2,1)S(1)} %pad_maximum_fusion), channel_id=1, source_target_pairs={{0,16},{4,20},{8,24},{12,28},{16,32},{20,36},{24,40},{28,44},{32,4... | collective-permute-start | bytes 368648 | tf_op jit(solution)/shard_map/ppermute | solution.py:19
  200.3 19.2 %collective-permute-start.5 = (bf16[32,1920]{1,0:T(8,128)(2,1)S(1)}, bf16[32,1920]{1,0:T(8,128)(2,1)S(1)}, u32[]{:S(2)}, u32[]{:S(2)}) collective-permute-start(bf16[32,1920]{1,0:T(8,128)(2,1)S(1)} %pad_maximum_fusion), channel_id=1, source_target_pairs={{0,12},{4,16},{8,20},{12,24},{16,28},{20,32},{24,36},{28,40},{32,4... | collective-permute-start | bytes 368648 | tf_op jit(solution)/shard_map/ppermute | solution.py:19
  205.4 17.0 %collective-permute-start.6 = (bf16[32,1920]{1,0:T(8,128)(2,1)S(1)}, bf16[32,1920]{1,0:T(8,128)(2,1)S(1)}, u32[]{:S(2)}, u32[]{:S(2)}) collective-permute-start(bf16[32,1920]{1,0:T(8,128)(2,1)S(1)} %pad_maximum_fusion), channel_id=1, source_target_pairs={{0,8},{4,12},{8,16},{12,20},{16,24},{20,28},{24,32},{28,36},{32,40... | collective-permute-start | bytes 368648 | tf_op jit(solution)/shard_map/ppermute | solution.py:19
  208.6 15.0 %collective-permute-start.7 = (bf16[32,1920]{1,0:T(8,128)(2,1)S(1)}, bf16[32,1920]{1,0:T(8,128)(2,1)S(1)}, u32[]{:S(2)}, u32[]{:S(2)}) collective-permute-start(bf16[32,1920]{1,0:T(8,128)(2,1)S(1)} %pad_maximum_fusion), channel_id=1, source_target_pairs={{0,4},{4,8},{8,12},{12,16},{16,20},{20,24},{24,28},{28,32},{32,36}... | collective-permute-start | bytes 368648 | tf_op jit(solution)/shard_map/ppermute | solution.py:19
  210.6 14.5 %collective-permute-start.8 = (bf16[32,1920]{1,0:T(8,128)(2,1)S(1)}, bf16[32,1920]{1,0:T(8,128)(2,1)S(1)}, u32[]{:S(2)}, u32[]{:S(2)}) collective-permute-start(bf16[32,1920]{1,0:T(8,128)(2,1)S(1)} %pad_maximum_fusion), channel_id=1, source_target_pairs={{4,0},{8,4},{12,8},{16,12},{20,16},{24,20},{28,24},{32,28},{36,32}... | collective-permute-start | bytes 368648 | tf_op jit(solution)/shard_map/ppermute | solution.py:19
  213.7 12.7 %collective-permute-start.9 = (bf16[32,1920]{1,0:T(8,128)(2,1)S(1)}, bf16[32,1920]{1,0:T(8,128)(2,1)S(1)}, u32[]{:S(2)}, u32[]{:S(2)}) collective-permute-start(bf16[32,1920]{1,0:T(8,128)(2,1)S(1)} %pad_maximum_fusion), channel_id=1, source_target_pairs={{8,0},{12,4},{16,8},{20,12},{24,16},{28,20},{32,24},{36,28},{40,32... | collective-permute-start | bytes 368648 | tf_op jit(solution)/shard_map/ppermute | solution.py:19
  219.5 12.6 %collective-permute-start.10 = (bf16[32,1920]{1,0:T(8,128)(2,1)S(1)}, bf16[32,1920]{1,0:T(8,128)(2,1)S(1)}, u32[]{:S(2)}, u32[]{:S(2)}) collective-permute-start(bf16[32,1920]{1,0:T(8,128)(2,1)S(1)} %pad_maximum_fusion), channel_id=1, source_target_pairs={{12,0},{16,4},{20,8},{24,12},{28,16},{32,20},{36,24},{40,28},{44,3... | collective-permute-start | bytes 368648 | tf_op jit(solution)/shard_map/ppermute | solution.py:19
  222.3 15.2 %collective-permute-start.11 = (bf16[32,1920]{1,0:T(8,128)(2,1)S(1)}, bf16[32,1920]{1,0:T(8,128)(2,1)S(1)}, u32[]{:S(2)}, u32[]{:S(2)}) collective-permute-start(bf16[32,1920]{1,0:T(8,128)(2,1)S(1)} %pad_maximum_fusion), channel_id=1, source_target_pairs={{16,0},{20,4},{24,8},{28,12},{32,16},{36,20},{40,24},{44,28},{48,3... | collective-permute-start | bytes 368648 | tf_op jit(solution)/shard_map/ppermute | solution.py:19
  223.6 19.0 %collective-permute-start.12 = (bf16[32,1920]{1,0:T(8,128)(2,1)S(1)}, bf16[32,1920]{1,0:T(8,128)(2,1)S(1)}, u32[]{:S(2)}, u32[]{:S(2)}) collective-permute-start(bf16[32,1920]{1,0:T(8,128)(2,1)S(1)} %pad_maximum_fusion), channel_id=1, source_target_pairs={{20,0},{24,4},{28,8},{32,12},{36,16},{40,20},{44,24},{48,28},{52,3... | collective-permute-start | bytes 368648 | tf_op jit(solution)/shard_map/ppermute | solution.py:19
  225.1 20.1 %collective-permute-start.13 = (bf16[32,1920]{1,0:T(8,128)(2,1)S(1)}, bf16[32,1920]{1,0:T(8,128)(2,1)S(1)}, u32[]{:S(2)}, u32[]{:S(2)}) collective-permute-start(bf16[32,1920]{1,0:T(8,128)(2,1)S(1)} %pad_maximum_fusion), channel_id=1, source_target_pairs={{24,0},{28,4},{32,8},{36,12},{40,16},{44,20},{48,24},{52,28},{56,3... | collective-permute-start | bytes 368648 | tf_op jit(solution)/shard_map/ppermute | solution.py:19
  226.4 18.8 %collective-permute-start.14 = (bf16[32,1920]{1,0:T(8,128)(2,1)S(1)}, bf16[32,1920]{1,0:T(8,128)(2,1)S(1)}, u32[]{:S(2)}, u32[]{:S(2)}) collective-permute-start(bf16[32,1920]{1,0:T(8,128)(2,1)S(1)} %pad_maximum_fusion), channel_id=1, source_target_pairs={{28,0},{32,4},{36,8},{40,12},{44,16},{48,20},{52,24},{56,28},{60,3... | collective-permute-start | bytes 368648 | tf_op jit(solution)/shard_map/ppermute | solution.py:19
  232.0 13.2 %collective-permute-start.15 = (bf16[32,1920]{1,0:T(8,128)(2,1)S(1)}, bf16[32,1920]{1,0:T(8,128)(2,1)S(1)}, u32[]{:S(2)}, u32[]{:S(2)}) collective-permute-start(bf16[32,1920]{1,0:T(8,128)(2,1)S(1)} %pad_maximum_fusion), channel_id=1, source_target_pairs={{32,0},{36,4},{40,8},{44,12},{48,16},{52,20},{56,24},{60,28},{64,3... | collective-permute-start | bytes 368648 | tf_op jit(solution)/shard_map/ppermute | solution.py:19
Sparse Core Ops, SparseCore 0:
  318.0 51.4 reduce-scatter.1
where the time goes:
time: 380 us; the launch traced here: 378 us
  other arithmetic  179 us (47%)
  waiting for transfers between devices  74.5 us (20%)
  starting transfers between devices  46.2 us (12%)
  matrix products  38 us (10%)
  local copies, waits for them, and re-layouts  22.1 us (6%)
  between operations  14.4 us (4%)
  loops' own time  3.82 us (1%)
    another operation x16, other arithmetic  144 us
    reduce_scatter x1, waiting for transfers between devices, shards(): lax.psum_scatter(pieces.reshape(lax.axis_size('cuts') * quarter, cross.sh...  51.6 us
    ppermute x16, starting transfers between devices, shifted(): lax.ppermute(value, axis, [(source, source + steps) for source in range(l...  46.2 us
    mul x4, other arithmetic, lag_table(): jnp.cos(angles) * scale  31.4 us
    ppermute x16, waiting for transfers between devices, shifted(): lax.ppermute(value, axis, [(source, source + steps) for source in range(l...  22.8 us
    dot_general x16, matrix products, advance(): jnp.dot(piece, band_table(turn * block_len, block_len), preferred_element...  21.9 us
    dynamic_update_slice x8, local copies, waits for them, and re-layouts, shards(): lax.map(one_block, jnp.arange(lax.axis_size('cuts') * quarter // quarter,...  16.8 us
    dot_general x4, matrix products, lag_rows(): jnp.einsum('pcf,ft->tpc', spectra, lag_table(lag_begin, lag_count), preci...  12.6 us
  transfers between devices with their start and end apart: 17, of which 8 were waited for; matrix products, arithmetic and copies ran while one was open for 0% of the time, Pallas kernels for 0%

commit v1 on v0

v1 whole, which is shorter than its diff:
```python
import math

import jax
import jax.numpy as jnp
import ml_dtypes
import numpy as np
from jax import lax
from jax.experimental import pallas as pl
from jax.experimental.pallas import tpu as pltpu
from jax.sharding import PartitionSpec as P

SAMP = 8192
F0 = 32
NF = 960
SMOOTH = 32
PAIRS = 6
CHAN = 32
SLICES = 4
HOPS = 4
SLOTS = 2 * (2 * HOPS + 1)
MESH = pl.DeviceIdType.MESH
F32 = jnp.float32
BF16 = jnp.bfloat16
ROOT_HALF = math.sqrt(0.5)


def tables():
    n2 = np.arange(1024)
    k2 = np.arange(128)
    angle = 2 * np.pi * ((n2[:, None] * k2[None, :]) % 1024) / 1024
    forward = np.concatenate([np.cos(angle), np.sin(angle)], axis=1).astype(ml_dtypes.bfloat16)
    k1 = np.arange(8)
    angle = 2 * np.pi * k1[:, None] * n2[None, :] / SAMP
    forward_turn = np.concatenate([np.cos(angle), np.sin(angle)], axis=0).astype(np.float32)
    t1 = np.arange(256)
    angle = 2 * np.pi * ((k2[:, None] * t1[None, :]) % 256) / 256
    c, s = np.cos(angle), np.sin(angle)
    lag = np.block([[c, s], [-s, c]]).astype(ml_dtypes.bfloat16)
    angle = 2 * np.pi * k1[:, None] * t1[None, :] / 2048
    gain = ((-1.0) ** k1)[:, None] / math.sqrt(NF)
    turn = np.stack([np.cos(angle) * gain, np.sin(angle) * gain])
    turn = np.repeat(turn.reshape(2, 2, 4, 1, 256), 4, axis=3)
    lag_turn = turn.transpose(0, 2, 1, 3, 4).reshape(2, 4, 8, 256).astype(np.float32)
    bins = np.arange(NF)
    count = np.minimum(bins + SMOOTH, NF - 1) - np.maximum(bins - SMOOTH, 0) + 1
    inverse = np.ones(1024)
    inverse[F0 : F0 + NF] = 1.0 / count
    inverse = inverse.reshape(128, 8).T.astype(np.float32)
    return forward, forward_turn, lag, lag_turn, inverse


def kernel(
    x_ref,
    taper_ref,
    inverse_ref,
    fturn_ref,
    ftab_ref,
    ltab_ref,
    lturn_ref,
    pairs_ref,
    count_ref,
    out_ref,
    y_ref,
    stage0,
    stage1,
    win0,
    win1,
    lhs_ref,
    send0,
    send1,
    land0,
    land1,
    swap_send,
    swap_recv,
    hop_send,
    hop_recv,
    core_send,
    core_recv,
    back_send,
    back_recv,
):
    stage, win, sbuf, land = (stage0, stage1), (win0, win1), (send0, send1), (land0, land1)
    blocks = lax.axis_size("chan")
    me = lax.axis_index("chan")
    cut = lax.axis_index("cuts")
    core = lax.rem(me, 2)
    right = lax.rem(me + 2, blocks)
    left = lax.rem(me + blocks - 2, blocks)
    other = me + 1 - 2 * core

    def at(chan, cuts):
        return {"chan": chan, "cuts": cuts}

    def peer(j):
        return lax.rem(cut + j, SLICES)

    def slot(d):
        return 2 * (d + HOPS) + core

    barrier = pltpu.get_barrier_semaphore()
    for target in [at(right, cut), at(left, cut), at(other, cut)] + [at(me, peer(j)) for j in (1, 2, 3)]:
        pl.semaphore_signal(barrier, inc=1, device_id=target, device_id_type=MESH)

    def butterflies(j, carry):
        o = pl.multiple_of(j * 128, 128)
        x = [x_ref[:, pl.ds(pl.multiple_of(n1 * 1024 + o, 128), 128)].astype(F32) for n1 in range(8)]
        s = [x[n] + x[n + 4] for n in range(4)]
        d = [x[n] - x[n + 4] for n in range(4)]
        e0, e1 = s[0] + s[2], s[1] + s[3]
        dm, dp = (d[1] - d[3]) * ROOT_HALF, (d[1] + d[3]) * ROOT_HALF
        z1 = (d[0] + dm, -(d[2] + dp))
        z3 = (d[0] - dm, d[2] - dp)
        z2 = (s[0] - s[2], s[3] - s[1])
        y_ref[0:32, pl.ds(o, 128)] = (e0 + e1).astype(BF16)
        z = {1: z1, 2: z2, 3: z3, 4: (e0 - e1, None), 5: (z3[0], -z3[1]), 6: (z2[0], -z2[1]), 7: (z1[0], -z1[1])}
        for k1 in range(1, 8):
            c = fturn_ref[k1 : k1 + 1, pl.ds(o, 128)]
            q = fturn_ref[8 + k1 : 9 + k1, pl.ds(o, 128)]
            re, im = z[k1]
            if im is None:
                yr, yi = re * c, -(re * q)
            else:
                yr, yi = re * c + im * q, im * c - re * q
            base = 32 + 64 * (k1 - 1)
            y_ref[base : base + 32, pl.ds(o, 128)] = yr.astype(BF16)
            y_ref[base + 32 : base + 64, pl.ds(o, 128)] = yi.astype(BF16)
        return carry

    lax.fori_loop(0, 8, butterflies, 0)
    r = jnp.dot(y_ref[...], ftab_ref[...], preferred_element_type=F32)
    re = [r[0:32, :128]]
    im = [-r[0:32, 128:]]
    for k1 in range(1, 8):
        base = 32 + 64 * (k1 - 1)
        a, b = r[base : base + 32], r[base + 32 : base + 64]
        re.append(a[:, :128] + b[:, 128:])
        im.append(b[:, :128] - a[:, 128:])

    lane = lax.broadcasted_iota(jnp.int32, (CHAN, 128), 1)
    valid = (lane >= F0 // 8) & (lane < (F0 + NF) // 8)
    mag = [jnp.where(valid, jnp.sqrt(re[k] * re[k] + im[k] * im[k]), 0.0) for k in range(8)]
    low = [mag[0]]
    for k in range(1, 8):
        low.append(low[-1] + mag[k])
    high = [mag[7]]
    for k in range(6, -1, -1):
        high.append(high[-1] + mag[k])
    high = high[::-1]
    total = low[7]
    middle = total
    for step in range(1, 4):
        middle = middle + pltpu.roll(total, step, 1) + pltpu.roll(total, 128 - step, 1)
    upper = lax.broadcasted_iota(jnp.int32, (4, 8, 128), 1) < 4
    for k in range(8):
        level = (middle + pltpu.roll(high[k], 4, 1) + pltpu.roll(low[k], 124, 1)) * inverse_ref[k : k + 1, :]
        factor = taper_ref[k : k + 1, :] / (level + 1e-6)
        re[k] = (re[k] * factor).reshape(4, 8, 128)
        im[k] = (im[k] * factor).reshape(4, 8, 128)
    for k in range(4):
        for h in range(2):
            rows = []
            for part in (re, im):
                a, b = part[k], part[k + 4]
                if h == 0:
                    rows.append(jnp.where(upper, a, pltpu.roll(b, 4, 1)))
                else:
                    rows.append(jnp.where(upper, pltpu.roll(a, 4, 1), b))
            stage[h][:, :, k * 128 : (k + 1) * 128] = jnp.concatenate(rows, axis=1).astype(BF16)

    pl.semaphore_wait(barrier, 6)

    def swap(h, j):
        return pltpu.make_async_remote_copy(
            src_ref=stage[h].at[peer(j)],
            dst_ref=win[h].at[slot(0), cut],
            send_sem=swap_send.at[h, j - 1],
            recv_sem=swap_recv.at[h, j - 1],
            device_id=at(me, peer(j)),
            device_id_type=MESH,
        )

    def hop(h, way, step):
        sign = -1 if way == 0 else 1
        return pltpu.make_async_remote_copy(
            src_ref=win[h].at[slot(sign * (step - 1))],
            dst_ref=win[h].at[slot(sign * step)],
            send_sem=hop_send.at[h, way, step - 1],
            recv_sem=hop_recv.at[h, way, step - 1],
            device_id=at(right if way == 0 else left, cut),
            device_id_type=MESH,
        )

    def across(h, n):
        d = HOPS - 2 * HOPS * core if n == 7 else (0, -1, 1, -2, 2, -3, 3)[n]
        return pltpu.make_async_remote_copy(
            src_ref=win[h].at[slot(d)],
            dst_ref=win[h].at[slot(d)],
            send_sem=core_send.at[h, n],
            recv_sem=core_recv.at[h, n],
            device_id=at(other, cut),
            device_id_type=MESH,
        )

    def back(h, j):
        return pltpu.make_async_remote_copy(
            src_ref=sbuf[h].at[peer(j)],
            dst_ref=land[h].at[cut],
            send_sem=back_send.at[h, j - 1],
            recv_sem=back_recv.at[h, j - 1],
            device_id=at(me, peer(j)),
            device_id_type=MESH,
        )

    sublane = lax.broadcasted_iota(jnp.int32, (1, 8, 1), 1) < 4

    def correlate(h):
        first = me - core

        def pair(p):
            live = jnp.where(p < count_ref[0], 1.0, 0.0).astype(F32)
            a_slot = jnp.clip(pairs_ref[0, p] - first + 2 * HOPS, 0, SLOTS - 1)
            b_slot = jnp.clip(pairs_ref[1, p] - first + 2 * HOPS, 0, SLOTS - 1)
            cr = ci = None
            for s in range(SLICES):
                a = win[h][a_slot, s].astype(F32)
                b = win[h][b_slot, s].astype(F32)
                ar, ai, br, bi = a[:8], a[8:], b[:8], b[8:]
                tr, ti = ar * br + ai * bi, ai * br - ar * bi
                cr, ci = (tr, ti) if cr is None else (cr + tr, ci + ti)
            return cr * live, ci * live

        def two(q, carry):
            cr0, ci0 = pair(2 * q)
            cr1, ci1 = pair(2 * q + 1)
            cr = jnp.concatenate([cr0, cr1], axis=0).astype(BF16)
            ci = jnp.concatenate([ci0, ci1], axis=0).astype(BF16)
            rows = pl.ds(pl.multiple_of(16 * q, 16), 16)
            for k in range(4):
                lhs_ref[k, rows, 0:128] = cr[:, k * 128 : (k + 1) * 128]
                lhs_ref[k, rows, 128:256] = ci[:, k * 128 : (k + 1) * 128]
            return carry

        lax.fori_loop(0, PAIRS // 2, two, 0)
        v = jnp.dot(lhs_ref[...].reshape(4 * 48, 256), ltab_ref[...], preferred_element_type=F32)
        parts = []
        for k in range(4):
            rows = v[48 * k : 48 * (k + 1)].reshape(PAIRS, 8, 512)
            dr, di = rows[:, :, :256], rows[:, :, 256:]
            c, s = lturn_ref[0, k][None], lturn_ref[1, k][None]
            tr, ti = dr * c - di * s, dr * s + di * c
            tr = jnp.where(sublane, tr, -tr) + pltpu.roll(tr, 4, 1)
            ti = jnp.where(sublane, ti, -ti) + pltpu.roll(ti, 4, 1)
            parts.append((tr, ti))
        r0 = parts[0][0]
        c1 = jnp.where(sublane, 1.0, ROOT_HALF)
        c3 = jnp.where(sublane, 1.0, -ROOT_HALF)
        s13 = jnp.where(sublane, 0.0, ROOT_HALF)
        r1, i1 = parts[1][0] * c1 - parts[1][1] * s13, parts[1][0] * s13 + parts[1][1] * c1
        r2 = jnp.where(sublane, parts[2][0], -parts[2][1])
        r3, i3 = parts[3][0] * c3 - parts[3][1] * s13, parts[3][0] * s13 + parts[3][1] * c3
        plus, minus, even, odd = r0 + r2, r0 - r2, r1 + r3, i1 - i3
        for m, value in enumerate((plus + even, minus - odd, plus - even, minus + odd)):
            sbuf[h][m] = value.reshape(48, 256).astype(BF16)
        for j in (1, 2, 3):
            back(h, j).start()
        land[h][cut] = sbuf[h][cut]

    for h in range(2):
        for j in (1, 2, 3):
            swap(h, j).start()
        win[h][slot(0), cut] = stage[h][cut]
    for h in range(2):
        for j in (1, 2, 3):
            swap(h, j).wait_recv()
        hop(h, 0, 1).start()
        hop(h, 1, 1).start()
        across(h, 0).start()
    for step in range(1, HOPS + 1):
        for h in range(2):
            for way in range(2):
                hop(h, way, step).wait_recv()
                if step < HOPS:
                    hop(h, way, step + 1).start()
                    across(h, 2 * step - 1 + way).start()
            if step == HOPS:
                across(h, 7).start()
                for n in range(8):
                    across(h, n).wait_recv()
                correlate(h)

    for h in range(2):
        for j in (1, 2, 3):
            back(h, j).wait_recv()
    top = lax.broadcasted_iota(jnp.int32, (8, 256), 0) < 4
    for p in range(PAIRS):
        for y in range(2):
            halves = []
            for x in (2 * y, 2 * y + 1):
                a = land[0][x, 16 * (p // 2) : 16 * (p // 2) + 16].astype(F32)[8 * (p % 2) : 8 * (p % 2) + 8]
                b = land[1][x, 16 * (p // 2) : 16 * (p // 2) + 16].astype(F32)[8 * (p % 2) : 8 * (p % 2) + 8]
                first = jnp.where(top, a, pltpu.roll(b, 4, 0))
                second = jnp.where(top, pltpu.roll(a, 4, 0), b)
                halves.append(jnp.concatenate([first, second], axis=1))
            base = 32 * p + 16 * y
            out_ref[base : base + 16, :] = jnp.concatenate(halves, axis=0).astype(BF16)

    for h in range(2):
        for j in (1, 2, 3):
            swap(h, j).wait_send()
            back(h, j).wait_send()
        for way in range(2):
            for step in range(1, HOPS + 1):
                hop(h, way, step).wait_send()
        for n in range(8):
            across(h, n).wait_send()


def shards(strain, band_taper, pair_list, pair_counts):
    forward, forward_turn, lag, lag_turn, inverse = (jnp.asarray(t) for t in tables())
    taper = jnp.pad(band_taper, (F0, 1024 - F0 - NF)).reshape(128, 8).T
    pairs = pair_list.transpose(0, 2, 1).reshape(2, PAIRS)
    vmem = pl.BlockSpec(memory_space=pltpu.VMEM)
    smem = pl.BlockSpec(memory_space=pltpu.SMEM)
    dma = pltpu.SemaphoreType.DMA
    window = pltpu.VMEM((SLOTS, SLICES, 16, 512), BF16)
    piece = pltpu.VMEM((SLICES, 16, 512), BF16)
    result = pltpu.VMEM((SLICES, 48, 256), BF16)
    stacks = pl.pallas_call(
        kernel,
        out_shape=jax.ShapeDtypeStruct((PAIRS * CHAN, 512), BF16),
        in_specs=[vmem] * 7 + [smem] * 2,
        out_specs=vmem,
        scratch_shapes=[
            pltpu.VMEM((480, 1024), BF16),
            piece,
            piece,
            window,
            window,
            pltpu.VMEM((4, 48, 256), BF16),
            result,
            result,
            result,
            result,
            dma((2, 3)),
            dma((2, 3)),
            dma((2, 2, HOPS)),
            dma((2, 2, HOPS)),
            dma((2, 8)),
            dma((2, 8)),
            dma((2, 3)),
            dma((2, 3)),
        ],
        compiler_params=pltpu.CompilerParams(
            collective_id=0, has_side_effects=True, vmem_limit_bytes=32 * 1024 * 1024
        ),
    )(strain.reshape(CHAN, SAMP), taper, inverse, forward_turn, forward, lag, lag_turn, pairs, pair_counts)
    return stacks.reshape(PAIRS, CHAN, 512).transpose(2, 0, 1)


def solution(mesh):
    in_specs = (P("cuts", "chan", None), P(), P("chan", None, None), P("chan"))
    out_specs = P("cuts", "chan", None)
    return jax.shard_map(shards, mesh=mesh, in_specs=in_specs, out_specs=out_specs, check_vma=False)
```

time: 380 us -> 49.2 us (0.13)
  other arithmetic: 179 us -> 0 us
  waiting for transfers between devices: 74.5 us -> 0 us
  starting transfers between devices: 46.2 us -> 0 us
  Pallas kernels: 0 us -> 43.5 us
  matrix products: 38 us -> 0 us
  local copies, waits for them, and re-layouts: 22.1 us -> 4.66 us
  between operations: 14.4 us -> 0.7 us
  loops' own time: 3.82 us -> 0 us
    another operation x16 -> x0, other arithmetic: 144 us -> none
    reduce_scatter x1 -> x0, waiting for transfers between devices: 51.6 us -> none  [shards(): lax.psum_scatter(pieces.reshape(lax.axis_size('cuts') * quarter, cross.sh...]
    ppermute x16 -> x0, starting transfers between devices: 46.2 us -> none  [shifted(): lax.ppermute(value, axis, [(source, source + steps) for source in range(l...]
    pallas_call x0 -> x1, Pallas kernels: none -> 43.5 us  [shards(): pl.pallas_call(kernel, out_shape=jax.ShapeDtypeStruct((PAIRS * CHAN, 512)...]
    dot_general x23 -> x0, matrix products: 38 us -> none  [the longest x16 21.9 us: advance(): jnp.dot(piece, band_table(turn * block_len, block_len), preferred_element...]
    mul x9 -> x0, other arithmetic: 31.8 us -> none  [the longest x4 31.4 us: lag_table(): jnp.cos(angles) * scale]
    ppermute x16 -> x0, waiting for transfers between devices: 22.8 us -> none  [shifted(): lax.ppermute(value, axis, [(source, source + steps) for source in range(l...]
    dynamic_update_slice x8 -> x0, local copies, waits for them, and re-layouts: 16.8 us -> none  [shards(): lax.map(one_block, jnp.arange(lax.axis_size('cuts') * quarter // quarter,...]
  transfers between devices with their start and end apart: 17 -> 0, of which waited for: 8 -> 0; matrix products, arithmetic and copies ran while one was open for 0% -> 0% of each run, Pallas kernels for 0% -> 0%
where the time goes in v1:
time: 49.2 us; the launch traced here: 48.9 us
  Pallas kernels  43.5 us (88%)
  local copies, waits for them, and re-layouts  4.66 us (9%)
  between operations  0.7 us (1%)
    pallas_call x1, Pallas kernels, shards(): pl.pallas_call(kernel, out_shape=jax.ShapeDtypeStruct((PAIRS * CHAN, 512)...  43.5 us
    unnamed x17, local copies, waits for them, and re-layouts  4.46 us

profile of v1, /device:TPU:1, one launch (start us, length us, event | category | flops | bytes accessed | tf_op | source)
XLA Modules:
  0.0 48.9 jit_solution(17065554833417597851)
XLA Ops:
  0.0 0.0 copy-start.7
  0.7 0.0 copy-done.7
  0.7 0.1 pad.4
  0.8 0.0 copy-start.3
  0.8 0.0 copy-start.4
  0.8 0.1 reshape.13
  0.9 0.0 copy-start.5
  0.9 0.0 copy-start.6
  0.9 0.7 %copy-done.3 = f32[2,4,8,256]{3,2,1,0:T(8,128)S(1)} copy-done((f32[2,4,8,256]{3,2,1,0:T(8,128)S(1)}, f32[2,4,8,256]{3,2,1,0:T(8,128)}, u32[]{:S(2)}) %copy-start.3) | copy-done | bytes 65560
  1.6 0.0 copy-done.4
  1.6 0.0 copy-done.5
  1.6 0.0 copy-done.6
  1.6 0.0 copy-start
  1.6 1.0 %copy-done = bf16[1,32,8192]{2,1,0:T(8,128)(2,1)S(1)} copy-done((bf16[1,32,8192]{2,1,0:T(8,128)(2,1)S(1)}, bf16[1,32,8192]{2,1,0:T(8,128)(2,1)}, u32[]{:S(2)}) %copy-start) | copy-done | bytes 524312
  2.7 0.0 copy-start.1
  2.7 1.0 %copy-done.1 = bf16[1024,256]{1,0:T(8,128)(2,1)S(1)} copy-done((bf16[1024,256]{1,0:T(8,128)(2,1)S(1)}, bf16[1024,256]{1,0:T(8,128)(2,1)}, u32[]{:S(2)}) %copy-start.1) | copy-done | bytes 524312
  3.7 0.0 copy-start.2
  3.7 0.9 %copy-done.2 = bf16[256,512]{1,0:T(8,128)(2,1)S(1)} copy-done((bf16[256,512]{1,0:T(8,128)(2,1)S(1)}, bf16[256,512]{1,0:T(8,128)(2,1)}, u32[]{:S(2)}) %copy-start.2) | copy-done | bytes 262168
  4.7 43.5 %shard_map.91 = bf16[192,512]{1,0:T(8,128)(2,1)S(1)} custom-call(bf16[32,8192]{1,0:T(8,128)(2,1)S(1)} %bitcast.9, f32[8,128]{1,0:T(8,128)S(1)} %bitcast.10, f32[8,128]{1,0:T(8,128)S(1)} %copy-done.5, f32[16,1024]{1,0:T(8,128)S(1)} %copy-done.4, bf16[1024,256]{1,0:T(8,128)(2,1)S(1)} %copy-done.1, bf16[256,512]{1,0:T(8,128)(2,1)S(1)} %copy-done.2, ...), custom_call_target="tpu_custom_call" | custom-call | tf_op jit(solution)/shard_map/pallas_call | solution.py:328
  48.2 0.7 %copy.13 = bf16[512,6,32]{0,2,1:T(8,128)(2,1)} copy(bf16[512,6,32]{0,2,1:T(8,128)(2,1)S(1)} %bitcast.8) | data formatting | bytes 393216
  (1 shorter events, 0.0 us)
Async XLA Ops:
  0.0 0.7 %copy-start.7 = (f32[960]{0:T(1024)S(1)}, f32[960]{0:T(1024)}, u32[]{:S(2)}) copy-start(f32[960]{0:T(1024)} %param.10) | copy-start | bytes 11524
  0.8 0.8 %copy-start.3 = (f32[2,4,8,256]{3,2,1,0:T(8,128)S(1)}, f32[2,4,8,256]{3,2,1,0:T(8,128)}, u32[]{:S(2)}) copy-start(f32[2,4,8,256]{3,2,1,0:T(8,128)} %constant.16.clone.lturn_ref) | copy-start | bytes 196612
  0.8 0.9 %copy-start.4 = (f32[16,1024]{1,0:T(8,128)S(1)}, f32[16,1024]{1,0:T(8,128)}, u32[]{:S(2)}) copy-start(f32[16,1024]{1,0:T(8,128)} %constant.14.clone.fturn_ref) | copy-start | bytes 196612
  0.9 0.8 %copy-start.5 = (f32[8,128]{1,0:T(8,128)S(1)}, f32[8,128]{1,0:T(8,128)}, u32[]{:S(2)}) copy-start(f32[8,128]{1,0:T(8,128)} %constant.17.clone.inverse_ref) | copy-start | bytes 12292
  0.9 0.7 %copy-start.6 = (s32[1,6,2]{1,2,0:T(2,128)S(1)}, s32[1,6,2]{1,2,0:T(2,128)}, u32[]{:S(2)}) copy-start(s32[1,6,2]{1,2,0:T(2,128)} %param.11) | copy-start | bytes 148
  1.6 1.0 %copy-start = (bf16[1,32,8192]{2,1,0:T(8,128)(2,1)S(1)}, bf16[1,32,8192]{2,1,0:T(8,128)(2,1)}, u32[]{:S(2)}) copy-start(bf16[1,32,8192]{2,1,0:T(8,128)(2,1)} %param.9) | copy-start | bytes 1572868
  2.7 1.0 %copy-start.1 = (bf16[1024,256]{1,0:T(8,128)(2,1)S(1)}, bf16[1024,256]{1,0:T(8,128)(2,1)}, u32[]{:S(2)}) copy-start(bf16[1024,256]{1,0:T(8,128)(2,1)} %constant.13.clone.ftab_ref) | copy-start | bytes 1572868
  3.7 0.9 %copy-start.2 = (bf16[256,512]{1,0:T(8,128)(2,1)S(1)}, bf16[256,512]{1,0:T(8,128)(2,1)}, u32[]{:S(2)}) copy-start(bf16[256,512]{1,0:T(8,128)(2,1)} %constant.15.clone.ltab_ref) | copy-start | bytes 786436

commit v2 on v1

v2 whole, which is shorter than its diff:
```python
import math

import jax
import jax.numpy as jnp
import ml_dtypes
import numpy as np
from jax import lax
from jax.experimental import pallas as pl
from jax.experimental.pallas import tpu as pltpu
from jax.sharding import PartitionSpec as P

SAMP = 8192
F0 = 32
NF = 960
SMOOTH = 32
PAIRS = 6
CHAN = 32
SLICES = 4
HOPS = 4
SLOTS = 2 * (2 * HOPS + 1)
MESH = pl.DeviceIdType.MESH
F32 = jnp.float32
BF16 = jnp.bfloat16
ROOT_HALF = math.sqrt(0.5)


def tables():
    n2 = np.arange(1024)
    k2 = np.arange(128)
    angle = 2 * np.pi * ((n2[:, None] * k2[None, :]) % 1024) / 1024
    forward = np.concatenate([np.cos(angle), np.sin(angle)], axis=1).astype(ml_dtypes.bfloat16)
    k1 = np.arange(8)
    angle = 2 * np.pi * k1[:, None] * n2[None, :] / SAMP
    forward_turn = np.concatenate([np.cos(angle), np.sin(angle)], axis=0).astype(np.float32)
    t1 = np.arange(256)
    angle = 2 * np.pi * ((k2[:, None] * t1[None, :]) % 256) / 256
    c, s = np.cos(angle), np.sin(angle)
    lag = np.block([[c, s], [-s, c]]).astype(ml_dtypes.bfloat16)
    angle = 2 * np.pi * k1[:, None] * t1[None, :] / 2048
    gain = ((-1.0) ** k1)[:, None] / math.sqrt(NF)
    turn = np.stack([np.cos(angle) * gain, np.sin(angle) * gain])
    turn = np.repeat(turn.reshape(2, 2, 4, 1, 256), 4, axis=3)
    lag_turn = turn.transpose(0, 2, 1, 3, 4).reshape(2, 4, 8, 256).astype(np.float32)
    bins = np.arange(NF)
    count = np.minimum(bins + SMOOTH, NF - 1) - np.maximum(bins - SMOOTH, 0) + 1
    inverse = np.ones(1024)
    inverse[F0 : F0 + NF] = 1.0 / count
    inverse = inverse.reshape(128, 8).T.astype(np.float32)
    return forward, forward_turn, lag, lag_turn, inverse


def kernel(
    x_hbm,
    taper_hbm,
    inverse_hbm,
    fturn_hbm,
    ftab_hbm,
    ltab_hbm,
    lturn_hbm,
    pairs_hbm,
    count_hbm,
    out_ref,
    x_ref,
    taper_ref,
    inverse_ref,
    fturn_ref,
    ftab_ref,
    ltab_ref,
    lturn_ref,
    my_pairs,
    my_count,
    its_pairs,
    its_count,
    y_ref,
    stage,
    win0,
    win1,
    win2,
    win3,
    cross_re,
    cross_im,
    lhs_ref,
    sbuf0,
    sbuf1,
    land,
    load_sem,
    list_send,
    list_recv,
    swap_send,
    swap_recv,
    hop_send,
    hop_recv,
    back_send,
    back_recv,
):
    win, sbuf = (win0, win1, win2, win3), (sbuf0, sbuf1)
    blocks = lax.axis_size("chan")
    me = lax.axis_index("chan")
    cut = lax.axis_index("cuts")
    core = lax.rem(me, 2)
    right = lax.rem(me + 2, blocks)
    left = lax.rem(me + blocks - 2, blocks)
    other = me + 1 - 2 * core

    def at(chan, cuts):
        return {"chan": chan, "cuts": cuts}

    def peer(i):
        return lax.rem(cut + i, SLICES)

    group = [(i, r) for i in range(SLICES) for r in range(2) if (i, r) != (0, 0)]

    def member(i, r):
        return at(other if r else me, peer(i))

    barrier = pltpu.get_barrier_semaphore()
    for target in [at(right, cut), at(left, cut)] + [member(i, r) for i, r in group]:
        pl.semaphore_signal(barrier, inc=1, device_id=target, device_id_type=MESH)

    loads = []
    for n, (src, dst) in enumerate(
        [
            (x_hbm, x_ref),
            (fturn_hbm, fturn_ref),
            (ftab_hbm, ftab_ref),
            (taper_hbm, taper_ref),
            (inverse_hbm, inverse_ref),
            (ltab_hbm, ltab_ref),
            (lturn_hbm, lturn_ref),
            (pairs_hbm, my_pairs),
            (count_hbm, my_count),
        ]
    ):
        loads.append(pltpu.make_async_copy(src, dst, load_sem.at[n]))
        loads[-1].start()

    def taper_rows():
        row = lax.broadcasted_iota(jnp.int32, (8, NF), 0)
        bins = lax.broadcasted_iota(jnp.int32, (8, NF), 1)
        rest = jnp.where(lax.rem(bins, 8) == row, jnp.broadcast_to(taper_ref[...], (8, NF)), 0.0)
        terms = []
        for _ in range(3):
            term = rest.astype(BF16)
            rest = rest - term.astype(F32)
            terms.append(term.astype(F32))
        terms.append(jnp.zeros_like(rest))
        bins = lax.broadcasted_iota(jnp.int32, (NF, 128), 0)
        lanes = lax.broadcasted_iota(jnp.int32, (NF, 128), 1)
        pick = jnp.where(bins // 8 == lanes - F0 // 8, 1.0, 0.0).astype(BF16)
        g = jnp.dot(jnp.concatenate(terms, axis=0).astype(BF16), pick, preferred_element_type=F32)
        return g[0:8] + g[8:16] + g[16:24]

    loads[3].wait()
    taper = taper_rows()

    def butterflies(j, carry):
        o = pl.multiple_of(j * 128, 128)
        x = [x_ref[:, pl.ds(pl.multiple_of(n1 * 1024 + o, 128), 128)].astype(F32) for n1 in range(8)]
        s = [x[n] + x[n + 4] for n in range(4)]
        d = [x[n] - x[n + 4] for n in range(4)]
        e0, e1 = s[0] + s[2], s[1] + s[3]
        dm, dp = (d[1] - d[3]) * ROOT_HALF, (d[1] + d[3]) * ROOT_HALF
        z1 = (d[0] + dm, -(d[2] + dp))
        z3 = (d[0] - dm, d[2] - dp)
        z2 = (s[0] - s[2], s[3] - s[1])
        y_ref[0:32, pl.ds(o, 128)] = (e0 + e1).astype(BF16)
        z = {1: z1, 2: z2, 3: z3, 4: (e0 - e1, None), 5: (z3[0], -z3[1]), 6: (z2[0], -z2[1]), 7: (z1[0], -z1[1])}
        for k1 in range(1, 8):
            c = fturn_ref[k1 : k1 + 1, pl.ds(o, 128)]
            q = fturn_ref[8 + k1 : 9 + k1, pl.ds(o, 128)]
            re, im = z[k1]
            if im is None:
                yr, yi = re * c, -(re * q)
            else:
                yr, yi = re * c + im * q, im * c - re * q
            base = 32 + 64 * (k1 - 1)
            y_ref[base : base + 32, pl.ds(o, 128)] = yr.astype(BF16)
            y_ref[base + 32 : base + 64, pl.ds(o, 128)] = yi.astype(BF16)
        return carry

    loads[0].wait()
    loads[1].wait()
    lax.fori_loop(0, 8, butterflies, 0)
    loads[2].wait()
    r = jnp.dot(y_ref[...], ftab_ref[...], preferred_element_type=F32)
    re = [r[0:32, :128]]
    im = [-r[0:32, 128:]]
    for k1 in range(1, 8):
        base = 32 + 64 * (k1 - 1)
        a, b = r[base : base + 32], r[base + 32 : base + 64]
        re.append(a[:, :128] + b[:, 128:])
        im.append(b[:, :128] - a[:, 128:])

    loads[4].wait()
    lane = lax.broadcasted_iota(jnp.int32, (CHAN, 128), 1)
    valid = (lane >= F0 // 8) & (lane < (F0 + NF) // 8)
    mag = [jnp.where(valid, jnp.sqrt(re[k] * re[k] + im[k] * im[k]), 0.0) for k in range(8)]
    low = [mag[0]]
    for k in range(1, 8):
        low.append(low[-1] + mag[k])
    high = [mag[7]]
    for k in range(6, -1, -1):
        high.append(high[-1] + mag[k])
    high = high[::-1]
    total = low[7]
    middle = total
    for step in range(1, 4):
        middle = middle + pltpu.roll(total, step, 1) + pltpu.roll(total, 128 - step, 1)
    upper = lax.broadcasted_iota(jnp.int32, (4, 8, 128), 1) < 4
    for k in range(8):
        level = (middle + pltpu.roll(high[k], 4, 1) + pltpu.roll(low[k], 124, 1)) * inverse_ref[k : k + 1, :]
        factor = taper[k : k + 1, :] / (level + 1e-6)
        re[k] = (re[k] * factor).reshape(4, 8, 128)
        im[k] = (im[k] * factor).reshape(4, 8, 128)
    for k in range(4):
        for h in range(2):
            rows = []
            for part in (re, im):
                a, b = part[k], part[k + 4]
                if h == 0:
                    rows.append(jnp.where(upper, a, pltpu.roll(b, 4, 1)))
                else:
                    rows.append(jnp.where(upper, pltpu.roll(a, 4, 1), b))
            stage[h, :, :, k * 128 : (k + 1) * 128] = jnp.concatenate(rows, axis=1).astype(BF16)

    pl.semaphore_wait(barrier, 9)

    def swap(i, r):
        return pltpu.make_async_remote_copy(
            src_ref=stage.at[1 - core if r else core, peer(i)],
            dst_ref=win[(SLICES - i) % SLICES].at[HOPS, core],
            send_sem=swap_send.at[i, r],
            recv_sem=swap_recv.at[i, r],
            device_id=member(i, r),
            device_id_type=MESH,
        )

    def hop(j, way, step):
        sign = -1 if way == 0 else 1
        return pltpu.make_async_remote_copy(
            src_ref=win[j].at[HOPS + sign * (step - 1)],
            dst_ref=win[j].at[HOPS + sign * step],
            send_sem=hop_send.at[j, way, step - 1],
            recv_sem=hop_recv.at[j, way, step - 1],
            device_id=at(right if way == 0 else left, cut),
            device_id_type=MESH,
        )

    def back(i, r):
        return pltpu.make_async_remote_copy(
            src_ref=sbuf[r].at[peer(i)],
            dst_ref=land.at[core, cut],
            send_sem=back_send.at[i, r],
            recv_sem=back_recv.at[i, r],
            device_id=member(i, r),
            device_id_type=MESH,
        )

    def lists(n):
        src, dst = ((pairs_hbm, its_pairs), (count_hbm, its_count))[n]
        return pltpu.make_async_remote_copy(
            src_ref=src,
            dst_ref=dst,
            send_sem=list_send.at[n],
            recv_sem=list_recv.at[n],
            device_id=at(other, cut),
            device_id_type=MESH,
        )

    order = (0, 1, 3, 2)
    swap(0, 1).start()
    for i in (3, 1, 2):
        for r in range(2):
            swap(i, r).start()
    win[0][HOPS, core] = stage[core, cut]
    for n in range(2):
        lists(n).start()
    for n in (5, 6, 7, 8):
        loads[n].wait()

    def add_slice(j, fresh):
        first = me - core

        def pair(p, carry):
            for r, pairs in ((0, my_pairs), (1, its_pairs)):
                a_slot = jnp.clip(pairs[0, p] - first + 2 * HOPS, 0, SLOTS - 1)
                b_slot = jnp.clip(pairs[1, p] - first + 2 * HOPS, 0, SLOTS - 1)
                a = win[j][a_slot // 2, lax.rem(a_slot, 2)].astype(F32)
                b = win[j][b_slot // 2, lax.rem(b_slot, 2)].astype(F32)
                ar, ai, br, bi = a[:8], a[8:], b[:8], b[8:]
                tr, ti = ar * br + ai * bi, ai * br - ar * bi
                if not fresh:
                    tr, ti = tr + cross_re[r, p], ti + cross_im[r, p]
                cross_re[r, p] = tr
                cross_im[r, p] = ti
            return carry

        lax.fori_loop(0, PAIRS, pair, 0)

    sublane = lax.broadcasted_iota(jnp.int32, (1, 8, 1), 1) < 4

    def correlate(r, count_ref):
        live = [jnp.where(p < count_ref[0], 1.0, 0.0).astype(F32) for p in range(PAIRS)]
        for q in range(PAIRS // 2):
            cr = jnp.concatenate([cross_re[r, 2 * q + e] * live[2 * q + e] for e in range(2)], axis=0).astype(BF16)
            ci = jnp.concatenate([cross_im[r, 2 * q + e] * live[2 * q + e] for e in range(2)], axis=0).astype(BF16)
            for k in range(4):
                lhs_ref[r, k, 16 * q : 16 * q + 16, 0:128] = cr[:, k * 128 : (k + 1) * 128]
                lhs_ref[r, k, 16 * q : 16 * q + 16, 128:256] = ci[:, k * 128 : (k + 1) * 128]
        v = jnp.dot(lhs_ref[r].reshape(4 * 48, 256), ltab_ref[...], preferred_element_type=F32)
        parts = []
        for k in range(4):
            rows = v[48 * k : 48 * (k + 1)].reshape(PAIRS, 8, 512)
            dr, di = rows[:, :, :256], rows[:, :, 256:]
            c, s = lturn_ref[0, k][None], lturn_ref[1, k][None]
            tr, ti = dr * c - di * s, dr * s + di * c
            tr = jnp.where(sublane, tr, -tr) + pltpu.roll(tr, 4, 1)
            ti = jnp.where(sublane, ti, -ti) + pltpu.roll(ti, 4, 1)
            parts.append((tr, ti))
        r0 = parts[0][0]
        c1 = jnp.where(sublane, 1.0, ROOT_HALF)
        c3 = jnp.where(sublane, 1.0, -ROOT_HALF)
        s13 = jnp.where(sublane, 0.0, ROOT_HALF)
        r1, i1 = parts[1][0] * c1 - parts[1][1] * s13, parts[1][0] * s13 + parts[1][1] * c1
        r2 = jnp.where(sublane, parts[2][0], -parts[2][1])
        r3, i3 = parts[3][0] * c3 - parts[3][1] * s13, parts[3][0] * s13 + parts[3][1] * c3
        plus, minus, even, odd = r0 + r2, r0 - r2, r1 + r3, i1 - i3
        for m, value in enumerate((plus + even, minus - odd, plus - even, minus + odd)):
            sbuf[r][m] = value.reshape(48, 256).astype(BF16)

    for j in order:
        if j == 0:
            swap(0, 1).wait_recv()
        else:
            swap(SLICES - j, 0).wait_recv()
            swap(SLICES - j, 1).wait_recv()
        hop(j, 0, 1).start()
        hop(j, 1, 1).start()
    for n in range(2):
        lists(n).wait_recv()
    for step in range(1, HOPS + 1):
        for j in order:
            for way in range(2):
                hop(j, way, step).wait_recv()
                if step < HOPS:
                    hop(j, way, step + 1).start()
            if step == HOPS:
                add_slice(j, j == order[0])
    correlate(1, its_count)
    for i in (2, 1, 3, 0):
        back(i, 1).start()
    correlate(0, my_count)
    for i in (2, 1, 3):
        back(i, 0).start()
    land[core, cut] = sbuf[0][cut]

    for i, r in group:
        back(i, r).wait_recv()
    top = lax.broadcasted_iota(jnp.int32, (8, 256), 0) < 4
    for p in range(PAIRS):
        for y in range(2):
            halves = []
            for x in (2 * y, 2 * y + 1):
                a = land[0, x, 16 * (p // 2) : 16 * (p // 2) + 16].astype(F32)[8 * (p % 2) : 8 * (p % 2) + 8]
                b = land[1, x, 16 * (p // 2) : 16 * (p // 2) + 16].astype(F32)[8 * (p % 2) : 8 * (p % 2) + 8]
                first = jnp.where(top, a, pltpu.roll(b, 4, 0))
                second = jnp.where(top, pltpu.roll(a, 4, 0), b)
                halves.append(jnp.concatenate([first, second], axis=1))
            base = 32 * p + 16 * y
            out_ref[base : base + 16, :] = jnp.concatenate(halves, axis=0).astype(BF16)

    for n in range(2):
        lists(n).wait_send()
    for i, r in group:
        swap(i, r).wait_send()
        back(i, r).wait_send()
    for j in range(SLICES):
        for way in range(2):
            for step in range(1, HOPS + 1):
                hop(j, way, step).wait_send()


def shards(strain, band_taper, pair_list, pair_counts):
    forward, forward_turn, lag, lag_turn, inverse = (jnp.asarray(t) for t in tables())
    pairs = pair_list.transpose(0, 2, 1).reshape(2, PAIRS)
    operands = (
        strain.reshape(CHAN, SAMP),
        band_taper.reshape(1, NF),
        inverse,
        forward_turn,
        forward,
        lag,
        lag_turn,
        pairs,
        pair_counts,
    )
    dma = pltpu.SemaphoreType.DMA
    window = pltpu.VMEM((2 * HOPS + 1, 2, 16, 512), BF16)
    result = pltpu.VMEM((SLICES, 48, 256), BF16)
    stacks = pl.pallas_call(
        kernel,
        out_shape=jax.ShapeDtypeStruct((PAIRS * CHAN, 512), BF16),
        in_specs=[pl.BlockSpec(memory_space=pl.ANY)] * len(operands),
        out_specs=pl.BlockSpec(memory_space=pltpu.VMEM),
        scratch_shapes=[pltpu.VMEM(v.shape, v.dtype) for v in operands[:7]]
        + [
            pltpu.SMEM((2, PAIRS), jnp.int32),
            pltpu.SMEM((1,), jnp.int32),
            pltpu.SMEM((2, PAIRS), jnp.int32),
            pltpu.SMEM((1,), jnp.int32),
            pltpu.VMEM((480, 1024), BF16),
            pltpu.VMEM((2, SLICES, 16, 512), BF16),
            window,
            window,
            window,
            window,
            pltpu.VMEM((2, PAIRS, 8, 512), F32),
            pltpu.VMEM((2, PAIRS, 8, 512), F32),
            pltpu.VMEM((2, 4, 48, 256), BF16),
            result,
            result,
            pltpu.VMEM((2, SLICES, 48, 256), BF16),
            dma((len(operands),)),
            dma((2,)),
            dma((2,)),
            dma((SLICES, 2)),
            dma((SLICES, 2)),
            dma((SLICES, 2, HOPS)),
            dma((SLICES, 2, HOPS)),
            dma((SLICES, 2)),
            dma((SLICES, 2)),
        ],
        compiler_params=pltpu.CompilerParams(
            collective_id=0, has_side_effects=True, vmem_limit_bytes=60 * 1024 * 1024
        ),
    )(*operands)
    return stacks.reshape(PAIRS, CHAN, 512).transpose(2, 0, 1)


def solution(mesh):
    in_specs = (P("cuts", "chan", None), P(), P("chan", None, None), P("chan"))
    out_specs = P("cuts", "chan", None)
    return jax.shard_map(shards, mesh=mesh, in_specs=in_specs, out_specs=out_specs, check_vma=False)
```

time: 49.2 us -> 44.7 us (0.909)
  local copies, waits for them, and re-layouts: 4.66 us -> 1.62 us
  Pallas kernels: 43.5 us -> 42.3 us
    unnamed x17 -> x1, local copies, waits for them, and re-layouts: 4.46 us -> 1.62 us
    pallas_call x1, Pallas kernels: 43.5 us -> 42.3 us  [shards(): pl.pallas_call(kernel, out_shape=jax.ShapeDtypeStruct((PAIRS * CHAN, 512)...]
where the time goes in v2:
time: 44.7 us; the launch traced here: 44.6 us
  Pallas kernels  42.3 us (95%)
  local copies, waits for them, and re-layouts  1.62 us (4%)
  between operations  0.66 us (1%)
    pallas_call x1, Pallas kernels, shards(): pl.pallas_call(kernel, out_shape=jax.ShapeDtypeStruct((PAIRS * CHAN, 512)...  42.3 us
    unnamed x1, local copies, waits for them, and re-layouts  1.62 us

profile of v2, /device:TPU:1, one launch (start us, length us, event | category | flops | bytes accessed | tf_op | source)
XLA Modules:
  0.0 44.6 jit_solution(3799631645549174850)
XLA Ops:
  0.7 42.3 %shard_map.91 = bf16[192,512]{1,0:T(8,128)(2,1)} custom-call(bf16[32,8192]{1,0:T(8,128)(2,1)} %bitcast.9, f32[1,960]{1,0:T(1,128)} %bitcast.10, f32[8,128]{1,0:T(8,128)} %constant.14.clone.inverse_hbm, f32[16,1024]{1,0:T(8,128)} %constant.11.clone.fturn_hbm, bf16[1024,256]{1,0:T(8,128)(2,1)} %constant.10.clone.ftab_hbm, ...), custom_call_target="tpu_custom_call" | custom-call | tf_op jit(solution)/shard_map/pallas_call | solution.py:400
  42.9 1.6 %copy.12 = bf16[512,6,32]{0,2,1:T(8,128)(2,1)} copy(bf16[512,6,32]{0,2,1:T(8,128)(2,1)} %bitcast.8) | data formatting | bytes 393216

commit v3 on v2

--- a/solution.py
+++ b/solution.py
@@ -98,8 +98,8 @@
     me = lax.axis_index("chan")
     cut = lax.axis_index("cuts")
     core = lax.rem(me, 2)
-    right = lax.rem(me + 2, blocks)
-    left = lax.rem(me + blocks - 2, blocks)
+    chip = me // 2
+    chips = blocks // 2
     other = me + 1 - 2 * core
 
     def at(chan, cuts):
@@ -114,8 +114,16 @@
         return at(other if r else me, peer(i))
 
     barrier = pltpu.get_barrier_semaphore()
-    for target in [at(right, cut), at(left, cut)] + [member(i, r) for i, r in group]:
-        pl.semaphore_signal(barrier, inc=1, device_id=target, device_id_type=MESH)
+    for i, r in group:
+        pl.semaphore_signal(barrier, inc=1, device_id=member(i, r), device_id_type=MESH)
+
+    @pl.when(chip + 1 < chips)
+    def _():
+        pl.semaphore_signal(barrier, inc=1, device_id=at(me + 2, cut), device_id_type=MESH)
+
+    @pl.when(chip >= 1)
+    def _():
+        pl.semaphore_signal(barrier, inc=1, device_id=at(me - 2, cut), device_id_type=MESH)
 
     loads = []
     for n, (src, dst) in enumerate(
@@ -223,7 +231,7 @@
                     rows.append(jnp.where(upper, pltpu.roll(a, 4, 1), b))
             stage[h, :, :, k * 128 : (k + 1) * 128] = jnp.concatenate(rows, axis=1).astype(BF16)
 
-    pl.semaphore_wait(barrier, 9)
+    pl.semaphore_wait(barrier, 7 + jnp.where(chip + 1 < chips, 1, 0) + jnp.where(chip >= 1, 1, 0))
 
     def swap(i, r):
         return pltpu.make_async_remote_copy(
@@ -242,9 +250,30 @@
             dst_ref=win[j].at[HOPS + sign * step],
             send_sem=hop_send.at[j, way, step - 1],
             recv_sem=hop_recv.at[j, way, step - 1],
-            device_id=at(right if way == 0 else left, cut),
+            device_id=at(me - 2 * sign, cut),
             device_id_type=MESH,
         )
+
+    def send_hop(j, way, step):
+        here = chip >= step - 1 if way == 0 else chip + step - 1 < chips
+        there = chip + 1 < chips if way == 0 else chip >= 1
+
+        @pl.when(here & there)
+        def _():
+            hop(j, way, step).start()
+
+    def end_hop(j, way, step):
+        here = chip >= step - 1 if way == 0 else chip + step - 1 < chips
+        there = chip + 1 < chips if way == 0 else chip >= 1
+
+        @pl.when(here & there)
+        def _():
+            hop(j, way, step).wait_send()
+
+    def take_hop(j, way, step):
+        @pl.when(chip >= step if way == 0 else chip + step < chips)
+        def _():
+            hop(j, way, step).wait_recv()
 
     def back(i, r):
         return pltpu.make_async_remote_copy(
@@ -334,16 +363,16 @@
         else:
             swap(SLICES - j, 0).wait_recv()
             swap(SLICES - j, 1).wait_recv()
-        hop(j, 0, 1).start()
-        hop(j, 1, 1).start()
+        send_hop(j, 0, 1)
+        send_hop(j, 1, 1)
     for n in range(2):
         lists(n).wait_recv()
     for step in range(1, HOPS + 1):
         for j in order:
             for way in range(2):
-                hop(j, way, step).wait_recv()
+                take_hop(j, way, step)
                 if step < HOPS:
-                    hop(j, way, step + 1).start()
+                    send_hop(j, way, step + 1)
             if step == HOPS:
                 add_slice(j, j == order[0])
     correlate(1, its_count)
@@ -377,7 +406,7 @@
     for j in range(SLICES):
         for way in range(2):
             for step in range(1, HOPS + 1):
-                hop(j, way, step).wait_send()
+                end_hop(j, way, step)
 
 
 def shards(strain, band_taper, pair_list, pair_counts):
@@ -400,7 +429,7 @@
     stacks = pl.pallas_call(
         kernel,
         out_shape=jax.ShapeDtypeStruct((PAIRS * CHAN, 512), BF16),
-        in_specs=[pl.BlockSpec(memory_space=pl.ANY)] * len(operands),
+        in_specs=[pl.BlockSpec(memory_space=pltpu.HBM)] * len(operands),
         out_specs=pl.BlockSpec(memory_space=pltpu.VMEM),
         scratch_shapes=[pltpu.VMEM(v.shape, v.dtype) for v in operands[:7]]
         + [

time: 44.7 us -> 36.3 us (0.81)
  the two profiles are of different devices: /device:TPU:1 before, /device:TPU:248 now
where the time goes in v3:
time: 36.3 us; the launch traced here: 36.2 us
  Pallas kernels  33.9 us (93%)
  local copies, waits for them, and re-layouts  1.62 us (4%)
  between operations  0.66 us (2%)
    pallas_call x1, Pallas kernels, shards(): pl.pallas_call(kernel, out_shape=jax.ShapeDtypeStruct((PAIRS * CHAN, 512)...  33.9 us
    unnamed x1, local copies, waits for them, and re-layouts  1.62 us

profile of v3, /device:TPU:248, one launch (start us, length us, event | category | flops | bytes accessed | tf_op | source)
XLA Modules:
  0.0 36.2 jit_solution(14556273775442268740)
XLA Ops:
  0.7 33.9 %shard_map.91 = bf16[192,512]{1,0:T(8,128)(2,1)} custom-call(bf16[32,8192]{1,0:T(8,128)(2,1)} %bitcast.9, f32[1,960]{1,0:T(1,128)} %bitcast.10, f32[8,128]{1,0:T(8,128)} %constant.14.clone.inverse_hbm, f32[16,1024]{1,0:T(8,128)} %constant.11.clone.fturn_hbm, bf16[1024,256]{1,0:T(8,128)(2,1)} %constant.10.clone.ftab_hbm, ...), custom_call_target="tpu_custom_call" | custom-call | tf_op jit(solution)/shard_map/pallas_call | solution.py:429
  34.5 1.6 %copy.12 = bf16[512,6,32]{0,2,1:T(8,128)(2,1)} copy(bf16[512,6,32]{0,2,1:T(8,128)(2,1)} %bitcast.8) | data formatting | bytes 393216

commit v4 on v3

--- a/solution.py
+++ b/solution.py
@@ -46,27 +46,27 @@
     inverse = np.ones(1024)
     inverse[F0 : F0 + NF] = 1.0 / count
     inverse = inverse.reshape(128, 8).T.astype(np.float32)
-    return forward, forward_turn, lag, lag_turn, inverse
+    narrow = np.concatenate([forward, lag[:, :256], lag[:, 256:]], axis=0)
+    wide = np.zeros((160, 1024), np.float32)
+    wide[:16] = forward_turn
+    wide[16:32] = lag_turn.transpose(0, 2, 1, 3).reshape(16, 1024)
+    wide[32:40, :128] = inverse
+    return narrow, wide
 
 
 def kernel(
     x_hbm,
     taper_hbm,
-    inverse_hbm,
-    fturn_hbm,
-    ftab_hbm,
-    ltab_hbm,
-    lturn_hbm,
+    narrow_hbm,
+    wide_hbm,
     pairs_hbm,
     count_hbm,
     out_ref,
     x_ref,
     taper_ref,
-    inverse_ref,
-    fturn_ref,
+    wide_ref,
     ftab_ref,
     ltab_ref,
-    lturn_ref,
     my_pairs,
     my_count,
     its_pairs,
@@ -88,6 +88,8 @@
     list_recv,
     swap_send,
     swap_recv,
+    near_send,
+    near_recv,
     hop_send,
     hop_recv,
     back_send,
@@ -113,28 +115,31 @@
     def member(i, r):
         return at(other if r else me, peer(i))
 
+    def beside(i, r, way):
+        return at((other if r else me) + (2, -2)[way], peer(i))
+
     barrier = pltpu.get_barrier_semaphore()
     for i, r in group:
         pl.semaphore_signal(barrier, inc=1, device_id=member(i, r), device_id_type=MESH)
 
-    @pl.when(chip + 1 < chips)
-    def _():
-        pl.semaphore_signal(barrier, inc=1, device_id=at(me + 2, cut), device_id_type=MESH)
-
-    @pl.when(chip >= 1)
-    def _():
-        pl.semaphore_signal(barrier, inc=1, device_id=at(me - 2, cut), device_id_type=MESH)
+    whole = [(i, r) for i in (0, 1, 3, 2) for r in range(2)]
+    reaches = (chip + 1 < chips, chip >= 1)
+    for way in range(2):
+
+        @pl.when(reaches[way])
+        def _(way=way):
+            for i, r in whole:
+                pl.semaphore_signal(barrier, inc=1, device_id=beside(i, r, way), device_id_type=MESH)
 
     loads = []
     for n, (src, dst) in enumerate(
         [
             (x_hbm, x_ref),
-            (fturn_hbm, fturn_ref),
-            (ftab_hbm, ftab_ref),
+            (wide_hbm.at[0:40], wide_ref),
+            (narrow_hbm.at[0:1024], ftab_ref),
             (taper_hbm, taper_ref),
-            (inverse_hbm, inverse_ref),
-            (ltab_hbm, ltab_ref),
-            (lturn_hbm, lturn_ref),
+            (narrow_hbm.at[1024:1280], ltab_ref.at[0]),
+            (narrow_hbm.at[1280:1536], ltab_ref.at[1]),
             (pairs_hbm, my_pairs),
             (count_hbm, my_count),
         ]
@@ -174,8 +179,8 @@
         y_ref[0:32, pl.ds(o, 128)] = (e0 + e1).astype(BF16)
         z = {1: z1, 2: z2, 3: z3, 4: (e0 - e1, None), 5: (z3[0], -z3[1]), 6: (z2[0], -z2[1]), 7: (z1[0], -z1[1])}
         for k1 in range(1, 8):
-            c = fturn_ref[k1 : k1 + 1, pl.ds(o, 128)]
-            q = fturn_ref[8 + k1 : 9 + k1, pl.ds(o, 128)]
+            c = wide_ref[k1 : k1 + 1, pl.ds(o, 128)]
+            q = wide_ref[8 + k1 : 9 + k1, pl.ds(o, 128)]
             re, im = z[k1]
             if im is None:
                 yr, yi = re * c, -(re * q)
@@ -199,7 +204,6 @@
         re.append(a[:, :128] + b[:, 128:])
         im.append(b[:, :128] - a[:, 128:])
 
-    loads[4].wait()
     lane = lax.broadcasted_iota(jnp.int32, (CHAN, 128), 1)
     valid = (lane >= F0 // 8) & (lane < (F0 + NF) // 8)
     mag = [jnp.where(valid, jnp.sqrt(re[k] * re[k] + im[k] * im[k]), 0.0) for k in range(8)]
@@ -216,7 +220,7 @@
         middle = middle + pltpu.roll(total, step, 1) + pltpu.roll(total, 128 - step, 1)
     upper = lax.broadcasted_iota(jnp.int32, (4, 8, 128), 1) < 4
     for k in range(8):
-        level = (middle + pltpu.roll(high[k], 4, 1) + pltpu.roll(low[k], 124, 1)) * inverse_ref[k : k + 1, :]
+        level = (middle + pltpu.roll(high[k], 4, 1) + pltpu.roll(low[k], 124, 1)) * wide_ref[32 + k : 33 + k, 0:128]
         factor = taper[k : k + 1, :] / (level + 1e-6)
         re[k] = (re[k] * factor).reshape(4, 8, 128)
         im[k] = (im[k] * factor).reshape(4, 8, 128)
@@ -231,7 +235,7 @@
                     rows.append(jnp.where(upper, pltpu.roll(a, 4, 1), b))
             stage[h, :, :, k * 128 : (k + 1) * 128] = jnp.concatenate(rows, axis=1).astype(BF16)
 
-    pl.semaphore_wait(barrier, 7 + jnp.where(chip + 1 < chips, 1, 0) + jnp.where(chip >= 1, 1, 0))
+    pl.semaphore_wait(barrier, 7 + jnp.where(reaches[0], 8, 0) + jnp.where(reaches[1], 8, 0))
 
     def swap(i, r):
         return pltpu.make_async_remote_copy(
@@ -243,37 +247,49 @@
             device_id_type=MESH,
         )
 
+    def near(i, r, way):
+        return pltpu.make_async_remote_copy(
+            src_ref=stage.at[1 - core if r else core, peer(i)],
+            dst_ref=win[(SLICES - i) % SLICES].at[HOPS + (-1, 1)[way], core],
+            send_sem=near_send.at[i, r, way],
+            recv_sem=near_recv.at[i, r, way],
+            device_id=beside(i, r, way),
+            device_id_type=MESH,
+        )
+
     def hop(j, way, step):
         sign = -1 if way == 0 else 1
         return pltpu.make_async_remote_copy(
             src_ref=win[j].at[HOPS + sign * (step - 1)],
             dst_ref=win[j].at[HOPS + sign * step],
-            send_sem=hop_send.at[j, way, step - 1],
-            recv_sem=hop_recv.at[j, way, step - 1],
+            send_sem=hop_send.at[j, way, step - 2],
+            recv_sem=hop_recv.at[j, way, step - 2],
             device_id=at(me - 2 * sign, cut),
             device_id_type=MESH,
         )
 
     def send_hop(j, way, step):
         here = chip >= step - 1 if way == 0 else chip + step - 1 < chips
-        there = chip + 1 < chips if way == 0 else chip >= 1
-
-        @pl.when(here & there)
+
+        @pl.when(here & reaches[way])
         def _():
             hop(j, way, step).start()
 
     def end_hop(j, way, step):
         here = chip >= step - 1 if way == 0 else chip + step - 1 < chips
-        there = chip + 1 < chips if way == 0 else chip >= 1
-
-        @pl.when(here & there)
+
+        @pl.when(here & reaches[way])
         def _():
             hop(j, way, step).wait_send()
 
     def take_hop(j, way, step):
         @pl.when(chip >= step if way == 0 else chip + step < chips)
         def _():
-            hop(j, way, step).wait_recv()
+            if step == 1:
+                for r in range(2):
+                    near((SLICES - j) % SLICES, r, way).wait_recv()
+            else:
+                hop(j, way, step).wait_recv()
 
     def back(i, r):
         return pltpu.make_async_remote_copy(
@@ -297,14 +313,20 @@
         )
 
     order = (0, 1, 3, 2)
-    swap(0, 1).start()
-    for i in (3, 1, 2):
-        for r in range(2):
-            swap(i, r).start()
+    for i in (0, 3, 1, 2):
+        for way in range(2):
+
+            @pl.when(reaches[way])
+            def _(way=way, i=i):
+                for r in range(2):
+                    near(i, r, way).start()
+
+    for i, r in group:
+        swap(i, r).start()
     win[0][HOPS, core] = stage[core, cut]
     for n in range(2):
         lists(n).start()
-    for n in (5, 6, 7, 8):
+    for n in (4, 5, 6, 7):
         loads[n].wait()
 
     def add_slice(j, fresh):
@@ -336,12 +358,15 @@
             for k in range(4):
                 lhs_ref[r, k, 16 * q : 16 * q + 16, 0:128] = cr[:, k * 128 : (k + 1) * 128]
                 lhs_ref[r, k, 16 * q : 16 * q + 16, 128:256] = ci[:, k * 128 : (k + 1) * 128]
-        v = jnp.dot(lhs_ref[r].reshape(4 * 48, 256), ltab_ref[...], preferred_element_type=F32)
+        lhs = lhs_ref[r].reshape(4 * 48, 256)
+        vr = jnp.dot(lhs, ltab_ref[0], preferred_element_type=F32)
+        vi = jnp.dot(lhs, ltab_ref[1], preferred_element_type=F32)
         parts = []
         for k in range(4):
-            rows = v[48 * k : 48 * (k + 1)].reshape(PAIRS, 8, 512)
-            dr, di = rows[:, :, :256], rows[:, :, 256:]
-            c, s = lturn_ref[0, k][None], lturn_ref[1, k][None]
+            dr = vr[48 * k : 48 * (k + 1)].reshape(PAIRS, 8, 256)
+            di = vi[48 * k : 48 * (k + 1)].reshape(PAIRS, 8, 256)
+            c = wide_ref[16:24, 256 * k : 256 * (k + 1)][None]
+            s = wide_ref[24:32, 256 * k : 256 * (k + 1)][None]
             tr, ti = dr * c - di * s, dr * s + di * c
             tr = jnp.where(sublane, tr, -tr) + pltpu.roll(tr, 4, 1)
             ti = jnp.where(sublane, ti, -ti) + pltpu.roll(ti, 4, 1)
@@ -357,17 +382,12 @@
         for m, value in enumerate((plus + even, minus - odd, plus - even, minus + odd)):
             sbuf[r][m] = value.reshape(48, 256).astype(BF16)
 
-    for j in order:
-        if j == 0:
-            swap(0, 1).wait_recv()
-        else:
-            swap(SLICES - j, 0).wait_recv()
-            swap(SLICES - j, 1).wait_recv()
-        send_hop(j, 0, 1)
-        send_hop(j, 1, 1)
-    for n in range(2):
-        lists(n).wait_recv()
     for step in range(1, HOPS + 1):
+        if step == 2:
+            for i, r in group:
+                swap(i, r).wait_recv()
+            for n in range(2):
+                lists(n).wait_recv()
         for j in order:
             for way in range(2):
                 take_hop(j, way, step)
@@ -405,21 +425,24 @@
         back(i, r).wait_send()
     for j in range(SLICES):
         for way in range(2):
-            for step in range(1, HOPS + 1):
+            for step in range(2, HOPS + 1):
                 end_hop(j, way, step)
+    for way in range(2):
+
+        @pl.when(reaches[way])
+        def _(way=way):
+            for i, r in whole:
+                near(i, r, way).wait_send()
 
 
 def shards(strain, band_taper, pair_list, pair_counts):
-    forward, forward_turn, lag, lag_turn, inverse = (jnp.asarray(t) for t in tables())
+    narrow, wide = (jnp.asarray(t) for t in tables())
     pairs = pair_list.transpose(0, 2, 1).reshape(2, PAIRS)
     operands = (
         strain.reshape(CHAN, SAMP),
         band_taper.reshape(1, NF),
-        inverse,
-        forward_turn,
-        forward,
-        lag,
-        lag_turn,
+        narrow,
+        wide,
         pairs,
         pair_counts,
     )
@@ -431,8 +454,12 @@
         out_shape=jax.ShapeDtypeStruct((PAIRS * CHAN, 512), BF16),
         in_specs=[pl.BlockSpec(memory_space=pltpu.HBM)] * len(operands),
         out_specs=pl.BlockSpec(memory_space=pltpu.VMEM),
-        scratch_shapes=[pltpu.VMEM(v.shape, v.dtype) for v in operands[:7]]
-        + [
+        scratch_shapes=[
+            pltpu.VMEM((CHAN, SAMP), BF16),
+            pltpu.VMEM((1, NF), F32),
+            pltpu.VMEM((40, 1024), F32),
+            pltpu.VMEM((1024, 256), BF16),
+            pltpu.VMEM((2, 256, 256), BF16),
             pltpu.SMEM((2, PAIRS), jnp.int32),
             pltpu.SMEM((1,), jnp.int32),
             pltpu.SMEM((2, PAIRS), jnp.int32),
@@ -449,20 +476,22 @@
             result,
             result,
             pltpu.VMEM((2, SLICES, 48, 256), BF16),
-            dma((len(operands),)),
+            dma((8,)),
             dma((2,)),
             dma((2,)),
             dma((SLICES, 2)),
             dma((SLICES, 2)),
-            dma((SLICES, 2, HOPS)),
-            dma((SLICES, 2, HOPS)),
+            dma((SLICES, 2, 2)),
+            dma((SLICES, 2, 2)),
+            dma((SLICES, 2, HOPS - 1)),
+            dma((SLICES, 2, HOPS - 1)),
             dma((SLICES, 2)),
             dma((SLICES, 2)),
         ],
         compiler_params=pltpu.CompilerParams(
-            collective_id=0, has_side_effects=True, vmem_limit_bytes=60 * 1024 * 1024
+            collective_id=0, has_side_effects=True, vmem_limit_bytes=48 * 1024 * 1024
         ),
-    )(*operands)
+    )(*(pltpu.with_memory_space_constraint(v, pltpu.HBM) for v in operands[:-1]), pair_counts)
     return stacks.reshape(PAIRS, CHAN, 512).transpose(2, 0, 1)
 
 

time: 36.3 us -> 34.1 us (0.939)
  Pallas kernels: 33.9 us -> 32.6 us
  local copies, waits for them, and re-layouts: 1.62 us -> 0.68 us
    pallas_call x1, Pallas kernels: 33.9 us -> 32.6 us  [shards(): pl.pallas_call(kernel, out_shape=jax.ShapeDtypeStruct((PAIRS * CHAN, 512)...]
    unnamed x1, local copies, waits for them, and re-layouts: 1.62 us -> 0.68 us
where the time goes in v4:
time: 34.1 us; the launch traced here: 34 us
  Pallas kernels  32.6 us (96%)
  local copies, waits for them, and re-layouts  0.68 us (2%)
  between operations  0.66 us (2%)
    pallas_call x1, Pallas kernels, shards(): pl.pallas_call(kernel, out_shape=jax.ShapeDtypeStruct((PAIRS * CHAN, 512)...  32.6 us

profile of v4, /device:TPU:248, one launch (start us, length us, event | category | flops | bytes accessed | tf_op | source)
XLA Modules:
  0.0 34.0 jit_solution(868298364516029823)
XLA Ops:
  0.7 32.6 %shard_map.64 = bf16[192,512]{1,0:T(8,128)(2,1)S(1)} custom-call(bf16[32,8192]{1,0:T(8,128)(2,1)} %bitcast.9, f32[1,960]{1,0:T(1,128)} %bitcast.10, bf16[1536,256]{1,0:T(8,128)(2,1)} %constant.4.clone.narrow_hbm, f32[160,1024]{1,0:T(8,128)} %constant.5.clone.wide_hbm, s32[2,6]{1,0:T(2,128)} %bitcast.11, s32[1]{0:T(128)S(6)} %copy.8.count_hbm), custom_call_target="tpu_custom_call" | custom-call | tf_op jit(solution)/shard_map/pallas_call | solution.py:452
  33.3 0.7 %copy.9 = bf16[512,6,32]{0,2,1:T(8,128)(2,1)} copy(bf16[512,6,32]{0,2,1:T(8,128)(2,1)S(1)} %bitcast.8) | data formatting | bytes 393216

commit v5 on v4

--- a/solution.py
+++ b/solution.py
@@ -17,6 +17,7 @@
 CHAN = 32
 SLICES = 4
 HOPS = 4
+ROW = 8
 SLOTS = 2 * (2 * HOPS + 1)
 MESH = pl.DeviceIdType.MESH
 F32 = jnp.float32
@@ -116,7 +117,7 @@
         return at(other if r else me, peer(i))
 
     def beside(i, r, way):
-        return at((other if r else me) + (2, -2)[way], peer(i))
+        return at((other if r else me) + 2 - 4 * way, peer(i))
 
     barrier = pltpu.get_barrier_semaphore()
     for i, r in group:
@@ -250,7 +251,7 @@
     def near(i, r, way):
         return pltpu.make_async_remote_copy(
             src_ref=stage.at[1 - core if r else core, peer(i)],
-            dst_ref=win[(SLICES - i) % SLICES].at[HOPS + (-1, 1)[way], core],
+            dst_ref=win[(SLICES - i) % SLICES].at[HOPS + 2 * way - 1, core],
             send_sem=near_send.at[i, r, way],
             recv_sem=near_recv.at[i, r, way],
             device_id=beside(i, r, way),
@@ -258,7 +259,7 @@
         )
 
     def hop(j, way, step):
-        sign = -1 if way == 0 else 1
+        sign = 2 * way - 1
         return pltpu.make_async_remote_copy(
             src_ref=win[j].at[HOPS + sign * (step - 1)],
             dst_ref=win[j].at[HOPS + sign * step],
@@ -268,28 +269,31 @@
             device_id_type=MESH,
         )
 
-    def send_hop(j, way, step):
-        here = chip >= step - 1 if way == 0 else chip + step - 1 < chips
-
-        @pl.when(here & reaches[way])
-        def _():
-            hop(j, way, step).start()
+    def comes(way, step):
+        return jnp.where(way == 0, chip, chips - 1 - chip) >= step
+
+    def goes(way, step):
+        return comes(way, step - 1) & (jnp.where(way == 0, chips - 1 - chip, chip) >= 1)
 
     def end_hop(j, way, step):
-        here = chip >= step - 1 if way == 0 else chip + step - 1 < chips
-
-        @pl.when(here & reaches[way])
+        @pl.when(goes(way, step))
         def _():
             hop(j, way, step).wait_send()
 
-    def take_hop(j, way, step):
-        @pl.when(chip >= step if way == 0 else chip + step < chips)
+    def take(j, way, step):
+        @pl.when(comes(way, step))
         def _():
             if step == 1:
                 for r in range(2):
                     near((SLICES - j) % SLICES, r, way).wait_recv()
             else:
                 hop(j, way, step).wait_recv()
+
+        if step < HOPS:
+
+            @pl.when(goes(way, step + 1))
+            def _():
+                hop(j, way, step + 1).start()
 
     def back(i, r):
         return pltpu.make_async_remote_copy(
@@ -382,19 +386,32 @@
         for m, value in enumerate((plus + even, minus - odd, plus - even, minus + odd)):
             sbuf[r][m] = value.reshape(48, 256).astype(BF16)
 
-    for step in range(1, HOPS + 1):
-        if step == 2:
+    row = lax.rem(chip, ROW)
+    sooner = jnp.where(row < 2, 1, 0)
+    later = 1 - sooner
+    behind = (row == 0) | (row == ROW - 1)
+    turns = [(step, j) for step in range(1, HOPS + 1) for j in order]
+    for n in range(len(turns) + 1):
+        if n == SLICES:
             for i, r in group:
                 swap(i, r).wait_recv()
-            for n in range(2):
-                lists(n).wait_recv()
-        for j in order:
-            for way in range(2):
-                take_hop(j, way, step)
-                if step < HOPS:
-                    send_hop(j, way, step + 1)
-            if step == HOPS:
-                add_slice(j, j == order[0])
+            for e in range(2):
+                lists(e).wait_recv()
+        if n < len(turns):
+            take(turns[n][1], sooner, turns[n][0])
+
+            @pl.when(jnp.logical_not(behind))
+            def _(n=n):
+                take(turns[n][1], later, turns[n][0])
+
+        if n > 0:
+
+            @pl.when(behind)
+            def _(n=n):
+                take(turns[n - 1][1], later, turns[n - 1][0])
+
+            if turns[n - 1][0] == HOPS:
+                add_slice(turns[n - 1][1], turns[n - 1][1] == order[0])
     correlate(1, its_count)
     for i in (2, 1, 3, 0):
         back(i, 1).start()

time: 34.1 us -> 32.3 us (0.947)
  Pallas kernels: 32.6 us -> 30.8 us
    pallas_call x1, Pallas kernels: 32.6 us -> 30.8 us  [shards(): pl.pallas_call(kernel, out_shape=jax.ShapeDtypeStruct((PAIRS * CHAN, 512)...]
where the time goes in v5:
time: 32.3 us; the launch traced here: 32.1 us
  Pallas kernels  30.8 us (95%)
  local copies, waits for them, and re-layouts  0.68 us (2%)
  between operations  0.66 us (2%)
    pallas_call x1, Pallas kernels, shards(): pl.pallas_call(kernel, out_shape=jax.ShapeDtypeStruct((PAIRS * CHAN, 512)...  30.8 us
    unnamed x1, local copies, waits for them, and re-layouts  0.68 us

profile of v5, /device:TPU:248, one launch (start us, length us, event | category | flops | bytes accessed | tf_op | source)
XLA Modules:
  0.0 32.1 jit_solution(6016435239648050084)
XLA Ops:
  0.7 30.8 %shard_map.64 = bf16[192,512]{1,0:T(8,128)(2,1)S(1)} custom-call(bf16[32,8192]{1,0:T(8,128)(2,1)} %bitcast.9, f32[1,960]{1,0:T(1,128)} %bitcast.10, bf16[1536,256]{1,0:T(8,128)(2,1)} %constant.4.clone.narrow_hbm, f32[160,1024]{1,0:T(8,128)} %constant.5.clone.wide_hbm, s32[2,6]{1,0:T(2,128)} %bitcast.11, s32[1]{0:T(128)S(6)} %copy.8.count_hbm), custom_call_target="tpu_custom_call" | custom-call | tf_op jit(solution)/shard_map/pallas_call | solution.py:469
  31.4 0.7 %copy.9 = bf16[512,6,32]{0,2,1:T(8,128)(2,1)} copy(bf16[512,6,32]{0,2,1:T(8,128)(2,1)S(1)} %bitcast.8) | data formatting | bytes 393216

commit v6 on v5

--- a/solution.py
+++ b/solution.py
@@ -73,6 +73,7 @@
     its_pairs,
     its_count,
     y_ref,
+    r_ref,
     stage,
     win0,
     win1,
@@ -120,33 +121,35 @@
         return at((other if r else me) + 2 - 4 * way, peer(i))
 
     barrier = pltpu.get_barrier_semaphore()
-    for i, r in group:
-        pl.semaphore_signal(barrier, inc=1, device_id=member(i, r), device_id_type=MESH)
-
-    whole = [(i, r) for i in (0, 1, 3, 2) for r in range(2)]
     reaches = (chip + 1 < chips, chip >= 1)
-    for way in range(2):
-
-        @pl.when(reaches[way])
-        def _(way=way):
-            for i, r in whole:
+    whole = [(i, r) for i in (2, 1, 3, 0) for r in range(2)]
+    for i, r in whole:
+        for way in range(2):
+
+            @pl.when(reaches[way])
+            def _(i=i, r=r, way=way):
                 pl.semaphore_signal(barrier, inc=1, device_id=beside(i, r, way), device_id_type=MESH)
+
+        if (i, r) in group:
+            pl.semaphore_signal(barrier, inc=1, device_id=member(i, r), device_id_type=MESH)
 
     loads = []
     for n, (src, dst) in enumerate(
         [
-            (x_hbm, x_ref),
+            (taper_hbm, taper_ref),
+            (x_hbm.at[0:16], x_ref.at[0:16]),
             (wide_hbm.at[0:40], wide_ref),
+            (x_hbm.at[16:32], x_ref.at[16:32]),
             (narrow_hbm.at[0:1024], ftab_ref),
-            (taper_hbm, taper_ref),
+            (pairs_hbm, my_pairs),
+            (count_hbm, my_count),
             (narrow_hbm.at[1024:1280], ltab_ref.at[0]),
             (narrow_hbm.at[1280:1536], ltab_ref.at[1]),
-            (pairs_hbm, my_pairs),
-            (count_hbm, my_count),
         ]
     ):
         loads.append(pltpu.make_async_copy(src, dst, load_sem.at[n]))
-        loads[-1].start()
+    for n in range(7):
+        loads[n].start()
 
     def taper_rows():
         row = lax.broadcasted_iota(jnp.int32, (8, NF), 0)
@@ -164,12 +167,13 @@
         g = jnp.dot(jnp.concatenate(terms, axis=0).astype(BF16), pick, preferred_element_type=F32)
         return g[0:8] + g[8:16] + g[16:24]
 
-    loads[3].wait()
+    loads[0].wait()
     taper = taper_rows()
 
-    def butterflies(j, carry):
+    def butterflies(first, j):
         o = pl.multiple_of(j * 128, 128)
-        x = [x_ref[:, pl.ds(pl.multiple_of(n1 * 1024 + o, 128), 128)].astype(F32) for n1 in range(8)]
+        rows = slice(first, first + 16)
+        x = [x_ref[rows, pl.ds(pl.multiple_of(n1 * 1024 + o, 128), 128)].astype(F32) for n1 in range(8)]
         s = [x[n] + x[n + 4] for n in range(4)]
         d = [x[n] - x[n + 4] for n in range(4)]
         e0, e1 = s[0] + s[2], s[1] + s[3]
@@ -177,7 +181,7 @@
         z1 = (d[0] + dm, -(d[2] + dp))
         z3 = (d[0] - dm, d[2] - dp)
         z2 = (s[0] - s[2], s[3] - s[1])
-        y_ref[0:32, pl.ds(o, 128)] = (e0 + e1).astype(BF16)
+        y_ref[first : first + 16, pl.ds(o, 128)] = (e0 + e1).astype(BF16)
         z = {1: z1, 2: z2, 3: z3, 4: (e0 - e1, None), 5: (z3[0], -z3[1]), 6: (z2[0], -z2[1]), 7: (z1[0], -z1[1])}
         for k1 in range(1, 8):
             c = wide_ref[k1 : k1 + 1, pl.ds(o, 128)]
@@ -187,60 +191,69 @@
                 yr, yi = re * c, -(re * q)
             else:
                 yr, yi = re * c + im * q, im * c - re * q
-            base = 32 + 64 * (k1 - 1)
-            y_ref[base : base + 32, pl.ds(o, 128)] = yr.astype(BF16)
-            y_ref[base + 32 : base + 64, pl.ds(o, 128)] = yi.astype(BF16)
-        return carry
-
-    loads[0].wait()
-    loads[1].wait()
-    lax.fori_loop(0, 8, butterflies, 0)
-    loads[2].wait()
-    r = jnp.dot(y_ref[...], ftab_ref[...], preferred_element_type=F32)
-    re = [r[0:32, :128]]
-    im = [-r[0:32, 128:]]
-    for k1 in range(1, 8):
-        base = 32 + 64 * (k1 - 1)
-        a, b = r[base : base + 32], r[base + 32 : base + 64]
-        re.append(a[:, :128] + b[:, 128:])
-        im.append(b[:, :128] - a[:, 128:])
-
-    lane = lax.broadcasted_iota(jnp.int32, (CHAN, 128), 1)
+            base = 32 + 64 * (k1 - 1) + first
+            y_ref[base : base + 16, pl.ds(o, 128)] = yr.astype(BF16)
+            y_ref[base + 32 : base + 48, pl.ds(o, 128)] = yi.astype(BF16)
+
+    for h in range(2):
+        loads[1 + 2 * h].wait()
+        if h == 0:
+            loads[2].wait()
+
+        def half(j, carry, h=h):
+            butterflies(16 * h, j)
+            return carry
+
+        lax.fori_loop(0, 8, half, 0)
+    loads[4].wait()
+    loads[7].start()
+    loads[8].start()
+    r_ref[...] = jnp.dot(y_ref[...], ftab_ref[...], preferred_element_type=F32)
+
+    lane = lax.broadcasted_iota(jnp.int32, (8, 128), 1)
     valid = (lane >= F0 // 8) & (lane < (F0 + NF) // 8)
-    mag = [jnp.where(valid, jnp.sqrt(re[k] * re[k] + im[k] * im[k]), 0.0) for k in range(8)]
-    low = [mag[0]]
-    for k in range(1, 8):
-        low.append(low[-1] + mag[k])
-    high = [mag[7]]
-    for k in range(6, -1, -1):
-        high.append(high[-1] + mag[k])
-    high = high[::-1]
-    total = low[7]
-    middle = total
-    for step in range(1, 4):
-        middle = middle + pltpu.roll(total, step, 1) + pltpu.roll(total, 128 - step, 1)
-    upper = lax.broadcasted_iota(jnp.int32, (4, 8, 128), 1) < 4
-    for k in range(8):
-        level = (middle + pltpu.roll(high[k], 4, 1) + pltpu.roll(low[k], 124, 1)) * wide_ref[32 + k : 33 + k, 0:128]
-        factor = taper[k : k + 1, :] / (level + 1e-6)
-        re[k] = (re[k] * factor).reshape(4, 8, 128)
-        im[k] = (im[k] * factor).reshape(4, 8, 128)
-    for k in range(4):
-        for h in range(2):
-            rows = []
-            for part in (re, im):
-                a, b = part[k], part[k + 4]
-                if h == 0:
-                    rows.append(jnp.where(upper, a, pltpu.roll(b, 4, 1)))
-                else:
-                    rows.append(jnp.where(upper, pltpu.roll(a, 4, 1), b))
-            stage[h, :, :, k * 128 : (k + 1) * 128] = jnp.concatenate(rows, axis=1).astype(BF16)
-
-    pl.semaphore_wait(barrier, 7 + jnp.where(reaches[0], 8, 0) + jnp.where(reaches[1], 8, 0))
+    upper = lax.broadcasted_iota(jnp.int32, (8, 128), 0) < 4
+
+    def whiten(i):
+        first = pl.multiple_of(8 * peer(i), 8)
+        low = r_ref[pl.ds(first, 8), :]
+        re, im = [low[:, :128]], [-low[:, 128:]]
+        for k1 in range(1, 8):
+            a = r_ref[pl.ds(first + 64 * k1 - 32, 8), :]
+            b = r_ref[pl.ds(first + 64 * k1, 8), :]
+            re.append(a[:, :128] + b[:, 128:])
+            im.append(b[:, :128] - a[:, 128:])
+        mag = [jnp.where(valid, jnp.sqrt(re[k] * re[k] + im[k] * im[k]), 0.0) for k in range(8)]
+        low = [mag[0]]
+        for k in range(1, 8):
+            low.append(low[-1] + mag[k])
+        high = [mag[7]]
+        for k in range(6, -1, -1):
+            high.append(high[-1] + mag[k])
+        high = high[::-1]
+        total = low[7]
+        middle = total
+        for step in range(1, 4):
+            middle = middle + pltpu.roll(total, step, 1) + pltpu.roll(total, 128 - step, 1)
+        for k in range(8):
+            level = (middle + pltpu.roll(high[k], 4, 1) + pltpu.roll(low[k], 124, 1)) * wide_ref[32 + k : 33 + k, 0:128]
+            factor = taper[k : k + 1, :] / (level + 1e-6)
+            re[k] = re[k] * factor
+            im[k] = im[k] * factor
+        for k in range(4):
+            for h in range(2):
+                rows = []
+                for part in (re, im):
+                    a, b = part[k], part[k + 4]
+                    if h == 0:
+                        rows.append(jnp.where(upper, a, pltpu.roll(b, 4, 0)))
+                    else:
+                        rows.append(jnp.where(upper, pltpu.roll(a, 4, 0), b))
+                stage[h, i, :, k * 128 : (k + 1) * 128] = jnp.concatenate(rows, axis=0).astype(BF16)
 
     def swap(i, r):
         return pltpu.make_async_remote_copy(
-            src_ref=stage.at[1 - core if r else core, peer(i)],
+            src_ref=stage.at[1 - core if r else core, i],
             dst_ref=win[(SLICES - i) % SLICES].at[HOPS, core],
             send_sem=swap_send.at[i, r],
             recv_sem=swap_recv.at[i, r],
@@ -250,7 +263,7 @@
 
     def near(i, r, way):
         return pltpu.make_async_remote_copy(
-            src_ref=stage.at[1 - core if r else core, peer(i)],
+            src_ref=stage.at[1 - core if r else core, i],
             dst_ref=win[(SLICES - i) % SLICES].at[HOPS + 2 * way - 1, core],
             send_sem=near_send.at[i, r, way],
             recv_sem=near_recv.at[i, r, way],
@@ -317,7 +330,10 @@
         )
 
     order = (0, 1, 3, 2)
-    for i in (0, 3, 1, 2):
+    for n, i in enumerate((0, 3, 1, 2)):
+        whiten(i)
+        if n == 0:
+            pl.semaphore_wait(barrier, 7 + jnp.where(reaches[0], 8, 0) + jnp.where(reaches[1], 8, 0))
         for way in range(2):
 
             @pl.when(reaches[way])
@@ -325,12 +341,10 @@
                 for r in range(2):
                     near(i, r, way).start()
 
-    for i, r in group:
-        swap(i, r).start()
-    win[0][HOPS, core] = stage[core, cut]
+    win[0][HOPS, core] = stage[core, 0]
     for n in range(2):
         lists(n).start()
-    for n in (4, 5, 6, 7):
+    for n in (5, 6, 7, 8):
         loads[n].wait()
 
     def add_slice(j, fresh):
@@ -392,11 +406,9 @@
     behind = (row == 0) | (row == ROW - 1)
     turns = [(step, j) for step in range(1, HOPS + 1) for j in order]
     for n in range(len(turns) + 1):
-        if n == SLICES:
+        if n == 8:
             for i, r in group:
-                swap(i, r).wait_recv()
-            for e in range(2):
-                lists(e).wait_recv()
+                swap(i, r).start()
         if n < len(turns):
             take(turns[n][1], sooner, turns[n][0])
 
@@ -411,6 +423,11 @@
                 take(turns[n - 1][1], later, turns[n - 1][0])
 
             if turns[n - 1][0] == HOPS:
+                if turns[n - 1][1] == order[0]:
+                    for i, r in group:
+                        swap(i, r).wait_recv()
+                    for e in range(2):
+                        lists(e).wait_recv()
                 add_slice(turns[n - 1][1], turns[n - 1][1] == order[0])
     correlate(1, its_count)
     for i in (2, 1, 3, 0):
@@ -482,6 +499,7 @@
             pltpu.SMEM((2, PAIRS), jnp.int32),
             pltpu.SMEM((1,), jnp.int32),
             pltpu.VMEM((480, 1024), BF16),
+            pltpu.VMEM((480, 256), F32),
             pltpu.VMEM((2, SLICES, 16, 512), BF16),
             window,
             window,
@@ -493,7 +511,7 @@
             result,
             result,
             pltpu.VMEM((2, SLICES, 48, 256), BF16),
-            dma((8,)),
+            dma((9,)),
             dma((2,)),
             dma((2,)),
             dma((SLICES, 2)),

time: 32.3 us -> 32.1 us (level)
  no operation moved by 1% of the time
where the time goes in v6:
time: 32.1 us; the launch traced here: 32 us
  Pallas kernels  30.6 us (95%)
  local copies, waits for them, and re-layouts  0.68 us (2%)
  between operations  0.66 us (2%)
    pallas_call x1, Pallas kernels, shards(): pl.pallas_call(kernel, out_shape=jax.ShapeDtypeStruct((PAIRS * CHAN, 512)...  30.6 us
    unnamed x1, local copies, waits for them, and re-layouts  0.68 us

profile of v6, /device:TPU:248, one launch (start us, length us, event | category | flops | bytes accessed | tf_op | source)
XLA Modules:
  0.0 32.0 jit_solution(12423736163502490745)
XLA Ops:
  0.7 30.6 %shard_map.64 = bf16[192,512]{1,0:T(8,128)(2,1)S(1)} custom-call(bf16[32,8192]{1,0:T(8,128)(2,1)} %bitcast.9, f32[1,960]{1,0:T(1,128)} %bitcast.10, bf16[1536,256]{1,0:T(8,128)(2,1)} %constant.4.clone.narrow_hbm, f32[160,1024]{1,0:T(8,128)} %constant.5.clone.wide_hbm, s32[2,6]{1,0:T(2,128)} %bitcast.11, s32[1]{0:T(128)S(6)} %copy.8.count_hbm), custom_call_target="tpu_custom_call" | custom-call | tf_op jit(solution)/shard_map/pallas_call | solution.py:486
  31.3 0.7 %copy.9 = bf16[512,6,32]{0,2,1:T(8,128)(2,1)} copy(bf16[512,6,32]{0,2,1:T(8,128)(2,1)S(1)} %bitcast.8) | data formatting | bytes 393216

commit v7 on v6

--- a/solution.py
+++ b/solution.py
@@ -170,6 +170,11 @@
     loads[0].wait()
     taper = taper_rows()
 
+    def put(row, o, value):
+        high = value.astype(BF16)
+        y_ref[row : row + 16, pl.ds(o, 128)] = high
+        y_ref[480 + row : 496 + row, pl.ds(o, 128)] = (value - high.astype(F32)).astype(BF16)
+
     def butterflies(first, j):
         o = pl.multiple_of(j * 128, 128)
         rows = slice(first, first + 16)
@@ -181,7 +186,7 @@
         z1 = (d[0] + dm, -(d[2] + dp))
         z3 = (d[0] - dm, d[2] - dp)
         z2 = (s[0] - s[2], s[3] - s[1])
-        y_ref[first : first + 16, pl.ds(o, 128)] = (e0 + e1).astype(BF16)
+        put(first, o, e0 + e1)
         z = {1: z1, 2: z2, 3: z3, 4: (e0 - e1, None), 5: (z3[0], -z3[1]), 6: (z2[0], -z2[1]), 7: (z1[0], -z1[1])}
         for k1 in range(1, 8):
             c = wide_ref[k1 : k1 + 1, pl.ds(o, 128)]
@@ -192,8 +197,8 @@
             else:
                 yr, yi = re * c + im * q, im * c - re * q
             base = 32 + 64 * (k1 - 1) + first
-            y_ref[base : base + 16, pl.ds(o, 128)] = yr.astype(BF16)
-            y_ref[base + 32 : base + 48, pl.ds(o, 128)] = yi.astype(BF16)
+            put(base, o, yr)
+            put(base + 32, o, yi)
 
     for h in range(2):
         loads[1 + 2 * h].wait()
@@ -208,7 +213,8 @@
     loads[4].wait()
     loads[7].start()
     loads[8].start()
-    r_ref[...] = jnp.dot(y_ref[...], ftab_ref[...], preferred_element_type=F32)
+    both = jnp.dot(y_ref[...], ftab_ref[...], preferred_element_type=F32)
+    r_ref[...] = both[:480] + both[480:]
 
     lane = lax.broadcasted_iota(jnp.int32, (8, 128), 1)
     valid = (lane >= F0 // 8) & (lane < (F0 + NF) // 8)
@@ -498,7 +504,7 @@
             pltpu.SMEM((1,), jnp.int32),
             pltpu.SMEM((2, PAIRS), jnp.int32),
             pltpu.SMEM((1,), jnp.int32),
-            pltpu.VMEM((480, 1024), BF16),
+            pltpu.VMEM((960, 1024), BF16),
             pltpu.VMEM((480, 256), F32),
             pltpu.VMEM((2, SLICES, 16, 512), BF16),
             window,

time: 32.1 us -> 32.1 us (level)
  no operation moved by 1% of the time
where the time goes in v7:
time: 32.1 us; the launch traced here: 31.9 us
  Pallas kernels  30.6 us (95%)
  local copies, waits for them, and re-layouts  0.68 us (2%)
  between operations  0.66 us (2%)
    pallas_call x1, Pallas kernels, shards(): pl.pallas_call(kernel, out_shape=jax.ShapeDtypeStruct((PAIRS * CHAN, 512)...  30.6 us
    unnamed x1, local copies, waits for them, and re-layouts  0.68 us

profile of v7, /device:TPU:248, one launch (start us, length us, event | category | flops | bytes accessed | tf_op | source)
XLA Modules:
  0.0 31.9 jit_solution(656748403742325741)
XLA Ops:
  0.7 30.6 %shard_map.64 = bf16[192,512]{1,0:T(8,128)(2,1)S(1)} custom-call(bf16[32,8192]{1,0:T(8,128)(2,1)} %bitcast.9, f32[1,960]{1,0:T(1,128)} %bitcast.10, bf16[1536,256]{1,0:T(8,128)(2,1)} %constant.4.clone.narrow_hbm, f32[160,1024]{1,0:T(8,128)} %constant.5.clone.wide_hbm, s32[2,6]{1,0:T(2,128)} %bitcast.11, s32[1]{0:T(128)S(6)} %copy.8.count_hbm), custom_call_target="tpu_custom_call" | custom-call | tf_op jit(solution)/shard_map/pallas_call | solution.py:492
  31.3 0.7 %copy.9 = bf16[512,6,32]{0,2,1:T(8,128)(2,1)} copy(bf16[512,6,32]{0,2,1:T(8,128)(2,1)S(1)} %bitcast.8) | data formatting | bytes 393216

commit v8 on v7

--- a/solution.py
+++ b/solution.py
@@ -436,11 +436,11 @@
                         lists(e).wait_recv()
                 add_slice(turns[n - 1][1], turns[n - 1][1] == order[0])
     correlate(1, its_count)
-    for i in (2, 1, 3, 0):
-        back(i, 1).start()
+    back(2, 1).start()
     correlate(0, my_count)
-    for i in (2, 1, 3):
-        back(i, 0).start()
+    back(2, 0).start()
+    for i, r in ((3, 1), (1, 1), (3, 0), (1, 0), (0, 1)):
+        back(i, r).start()
     land[core, cut] = sbuf[0][cut]
 
     for i, r in group:

time: 32.1 us -> 32.1 us (level)
  no operation moved by 1% of the time
where the time goes in v8:
time: 32.1 us; the launch traced here: 32 us
  Pallas kernels  30.6 us (95%)
  local copies, waits for them, and re-layouts  0.68 us (2%)
  between operations  0.66 us (2%)
    pallas_call x1, Pallas kernels, shards(): pl.pallas_call(kernel, out_shape=jax.ShapeDtypeStruct((PAIRS * CHAN, 512)...  30.6 us
    unnamed x1, local copies, waits for them, and re-layouts  0.68 us

profile of v8, /device:TPU:248, one launch (start us, length us, event | category | flops | bytes accessed | tf_op | source)
XLA Modules:
  0.0 32.0 jit_solution(12558957696646126922)
XLA Ops:
  0.7 30.6 %shard_map.64 = bf16[192,512]{1,0:T(8,128)(2,1)S(1)} custom-call(bf16[32,8192]{1,0:T(8,128)(2,1)} %bitcast.9, f32[1,960]{1,0:T(1,128)} %bitcast.10, bf16[1536,256]{1,0:T(8,128)(2,1)} %constant.4.clone.narrow_hbm, f32[160,1024]{1,0:T(8,128)} %constant.5.clone.wide_hbm, s32[2,6]{1,0:T(2,128)} %bitcast.11, s32[1]{0:T(128)S(6)} %copy.8.count_hbm), custom_call_target="tpu_custom_call" | custom-call | tf_op jit(solution)/shard_map/pallas_call | solution.py:492
  31.3 0.7 %copy.9 = bf16[512,6,32]{0,2,1:T(8,128)(2,1)} copy(bf16[512,6,32]{0,2,1:T(8,128)(2,1)S(1)} %bitcast.8) | data formatting | bytes 393216
